TPU v7x, 32 devices: a whole 2x2x4 slice. The times are simulated.
32 devices in a mesh: ctx: 4 (over y, core), fsdp: 8 (over z, x).
Axes of the slice: x: 2, y: 2, z: 4, core: 2. Of those that a mesh axis runs over, the one named last changes fastest.
Arguments:
- hidden: bfloat16 [4, 8, 256, 2048], P('ctx', 'fsdp'), may hold values from -4.5 to 4.5
- norm_gain: float32 [2048], replicated, may hold values from 0.1 to 1.9
- w_query: bfloat16 [2048, 2048], P('fsdp', 'ctx'), may hold values from -1 to 1
- w_key: bfloat16 [2048, 1024], P('fsdp', 'ctx'), may hold values from -1 to 1
- w_value: bfloat16 [2048, 1024], P('fsdp', 'ctx'), may hold values from -0.125 to 0.125
- q_gain: float32 [128], replicated, may hold values from 0.5 to 5
- k_gain: float32 [128], replicated, may hold values from 0.5 to 5
- lengths: int32 [8, 4], replicated, may hold values from 1 to 512, 1024 in all within a row
- piece_map: int32 [8, 4], replicated, may hold values from 0 to 3, each once within a row
- owner: int32 [4, 8, 256], P('ctx', 'fsdp'), may hold values from 0 to 31, as said below
- slot: int32 [4, 8, 256], P('ctx', 'fsdp'), may hold values from 0 to 511, as said below
Outputs:
- attended: bfloat16 [4, 8, 256, 2048], P('ctx', 'fsdp')
- cache: bfloat16 [16384, 2048], P(('ctx', 'fsdp'))
Inputs may be any that keep to these rules, and one draw needn't show every extreme that they name: `lengths`: each row sums to 1024; its largest entry is 512. `piece_map`: each row holds every piece once. At most 16 tokens of one device go to one owner; in every draw one owner receives exactly 16 from every device. `slot`: tokens with the same owner have distinct slots.
All inputs are finite; a program needn't handle non-finite values.
Results may differ from a plain program's by a relative error of at most 0.0035.
The roundings to bfloat16 on the way count: a program that leaves them out, or rounds other values in their place, can miss the bound.
Values may be sent and summed in bfloat16 or wider, within the bound.
A program may use at most 128 MiB of HBM per device.

v0:
```python
import math

import jax
import jax.numpy as jnp
from jax import lax
from jax.sharding import PartitionSpec as P

HEAD_WIDTH = 128


EPSILON = 1e-06
THETA = 1000000.0
NEG_BIG = -1e30


def norm_rope(projected, gain_vec, relative, head_size):
    row_count = projected.shape[0]
    head_count = projected.shape[1] // head_size
    shaped = projected.reshape(row_count, head_count, head_size)
    factor = lax.rsqrt(jnp.mean(shaped * shaped, axis=-1, keepdims=True) + EPSILON)
    normal = shaped * factor * gain_vec
    half_size = head_size // 2
    frequency = jnp.exp(
        jnp.arange(half_size, dtype=jnp.float32) * (-2.0 * math.log(THETA) / head_size)
    )
    angles = relative.astype(jnp.float32)[:, None] * frequency[None, :]
    cosine = jnp.cos(angles)[:, None, :]
    sine_part = jnp.sin(angles)[:, None, :]
    first_half = normal[..., :half_size]
    second = normal[..., half_size:]
    turned = jnp.concatenate(
        [first_half * cosine - second * sine_part, second * cosine + first_half * sine_part],
        axis=-1,
    )
    return turned.reshape(row_count, head_count * head_size).astype(jnp.bfloat16)


def attend_keys(
    state_tuple, heads_of_query, query_pos, query_seg, key_rows, value_rows, key_pos, key_seg
):
    row_max, row_sum, weighted = state_tuple
    heads_of_key = key_rows.reshape(key_rows.shape[0], -1, HEAD_WIDTH)
    heads_of_value = value_rows.reshape(value_rows.shape[0], -1, HEAD_WIDTH)
    scores = jnp.einsum(
        "tkgd,skd->tkgs", heads_of_query, heads_of_key, preferred_element_type=jnp.float32
    ) * (1.0 / math.sqrt(HEAD_WIDTH))
    visible = ((query_seg[:, None] == key_seg[None, :]) & (key_pos[None, :] <= query_pos[:, None]))[
        :, None, None, :
    ]
    masked = jnp.where(visible, scores, NEG_BIG)
    new_max = jnp.maximum(row_max, jnp.max(masked, axis=-1))
    weights = jnp.where(visible, jnp.exp(masked - new_max[..., None]), 0.0)
    shrink = jnp.exp(row_max - new_max)
    row_sum = row_sum * shrink + jnp.sum(weights, axis=-1)
    weighted = weighted * shrink[..., None] + jnp.einsum(
        "tkgs,skd->tkgd",
        weights.astype(jnp.bfloat16),
        heads_of_value,
        preferred_element_type=jnp.float32,
    )
    return (new_max, row_sum, weighted)


def sweep_keys(
    state_tuple, heads_of_query, query_pos, query_seg, key_rows, value_rows, key_pos, key_seg
):
    row_span = key_rows.shape[0]
    key_block = 512
    steps_count = row_span // key_block

    def step_keys(carried, key_items):
        return (
            attend_keys(
                carried,
                heads_of_query,
                query_pos,
                query_seg,
                key_items[0],
                key_items[1],
                key_items[2],
                key_items[3],
            ),
            None,
        )

    result_carry, unused = lax.scan(
        step_keys,
        state_tuple,
        (
            key_rows.reshape(steps_count, key_block, -1),
            value_rows.reshape(steps_count, key_block, -1),
            key_pos.reshape(steps_count, key_block),
            key_seg.reshape(steps_count, key_block),
        ),
    )
    return result_carry


def empty_state(row_count, kv_heads, group_width):
    return (
        jnp.full((row_count, kv_heads, group_width), NEG_BIG, jnp.float32),
        jnp.zeros((row_count, kv_heads, group_width), jnp.float32),
        jnp.zeros((row_count, kv_heads, group_width, HEAD_WIDTH), jnp.float32),
    )


def project_rows(source, pieces):
    return tuple(
        (jnp.dot(source, shard_rows, preferred_element_type=jnp.float32) for shard_rows in pieces)
    )


def shards(
    hidden, norm_gain, w_query, w_key, w_value, q_gain, k_gain, lengths, piece_map, owner, slot
):
    tok_rows = hidden.shape[2]
    ctx_count = lax.axis_size("ctx")
    fsdp_count = lax.axis_size("fsdp")
    owner_count = ctx_count * fsdp_count
    group_index = lax.axis_index("fsdp")
    ctx_index = lax.axis_index("ctx")
    inputs = hidden[0, 0].astype(jnp.float32)
    factor = lax.rsqrt(jnp.mean(inputs * inputs, axis=-1, keepdims=True) + EPSILON)
    normed = (inputs * factor * norm_gain).astype(jnp.bfloat16)
    my_lengths = lax.dynamic_index_in_dim(lengths, group_index, 0, keepdims=False)
    my_pieces = lax.dynamic_index_in_dim(piece_map, group_index, 0, keepdims=False)
    seg_ends = jnp.cumsum(my_lengths, dtype=jnp.int32)
    starts = seg_ends - my_lengths
    seg_count = lengths.shape[1]

    def stream_info(row_ids):
        holder = row_ids // tok_rows
        piece_ids = jnp.sum(
            jnp.where(
                holder[:, None] == jnp.arange(ctx_count, dtype=jnp.int32)[None, :],
                my_pieces[None, :],
                0,
            ),
            axis=1,
            dtype=jnp.int32,
        )
        positions = piece_ids * tok_rows + row_ids % tok_rows
        segment = jnp.sum(
            (positions[:, None] >= seg_ends[None, :]).astype(jnp.int32), axis=1, dtype=jnp.int32
        )
        relative = positions - jnp.sum(
            jnp.where(
                segment[:, None] == jnp.arange(seg_count, dtype=jnp.int32)[None, :],
                starts[None, :],
                0,
            ),
            axis=1,
            dtype=jnp.int32,
        )
        return (positions, segment, relative)

    query_cols, key_cols, value_cols = (
        lax.all_gather(w_query, "ctx", axis=1, tiled=True),
        lax.all_gather(w_key, "ctx", axis=1, tiled=True),
        lax.all_gather(w_value, "ctx", axis=1, tiled=True),
    )
    query_raw, key_raw, value_raw = project_rows(
        normed,
        (
            lax.all_gather(query_cols, "fsdp", axis=0, tiled=True),
            lax.all_gather(key_cols, "fsdp", axis=0, tiled=True),
            lax.all_gather(value_cols, "fsdp", axis=0, tiled=True),
        ),
    )
    own_ids = ctx_index * tok_rows + jnp.arange(tok_rows, dtype=jnp.int32)
    own_pos, own_seg, own_rel = stream_info(own_ids)
    query_rows = norm_rope(query_raw, q_gain, own_rel, HEAD_WIDTH)
    key_new = norm_rope(key_raw, k_gain, own_rel, HEAD_WIDTH)
    value_new = value_raw.astype(jnp.bfloat16)
    kv_heads = key_new.shape[1] // HEAD_WIDTH
    group_width = query_rows.shape[1] // key_new.shape[1]
    heads_of_query = query_rows.reshape(tok_rows, kv_heads, group_width, HEAD_WIDTH)
    pieces = (
        lax.all_gather(key_new, "ctx", axis=0, tiled=True),
        lax.all_gather(value_new, "ctx", axis=0, tiled=True),
    )
    row_ids = jnp.arange(pieces[0].shape[0], dtype=jnp.int32)
    key_pos, key_seg, unused = stream_info(row_ids)
    row_max, row_sum, weighted = sweep_keys(
        empty_state(tok_rows, kv_heads, group_width),
        heads_of_query,
        own_pos,
        own_seg,
        pieces[0],
        pieces[1],
        key_pos,
        key_seg,
    )
    attended = (weighted / row_sum[..., None]).reshape(tok_rows, -1).astype(jnp.bfloat16)
    kv_new = jnp.concatenate([key_new, value_new], axis=1)
    kv_width = kv_new.shape[1]
    per_owner = 2 * tok_rows // owner_count
    capacity = owner_count * per_owner
    own_owner = owner[0, 0]
    own_slot = slot[0, 0]
    onehot = (own_owner[:, None] == jnp.arange(owner_count, dtype=jnp.int32)[None, :]).astype(
        jnp.int32
    )
    rank_in_owner = jnp.sum(
        onehot * (jnp.cumsum(onehot, axis=0, dtype=jnp.int32) - 1), axis=1, dtype=jnp.int32
    )
    bucket_pos = own_owner * per_owner + rank_in_owner
    bucket = jnp.zeros((capacity, kv_width), jnp.bfloat16).at[bucket_pos].set(kv_new)
    bucket_slots = jnp.full((capacity,), capacity, jnp.int32).at[bucket_pos].set(own_slot)
    got_rows, got_slots = (
        lax.all_to_all(
            bucket.reshape(owner_count, per_owner, kv_width),
            ("ctx", "fsdp"),
            split_axis=0,
            concat_axis=0,
            tiled=True,
        ),
        lax.all_to_all(
            bucket_slots.reshape(owner_count, per_owner),
            ("ctx", "fsdp"),
            split_axis=0,
            concat_axis=0,
            tiled=True,
        ),
    )
    new_cache = (
        jnp.zeros((capacity, kv_width), jnp.bfloat16)
        .at[got_slots.reshape(-1)]
        .set(got_rows.reshape(-1, kv_width), mode="drop")
    )
    return (attended[None, None], new_cache)


def solution(mesh):
    placed = (
        P("ctx", "fsdp", None, None),
        P(),
        P("fsdp", "ctx"),
        P("fsdp", "ctx"),
        P("fsdp", "ctx"),
        P(),
        P(),
        P(),
        P(),
        P("ctx", "fsdp", None),
        P("ctx", "fsdp", None),
    )
    return jax.shard_map(
        shards,
        mesh=mesh,
        in_specs=placed,
        out_specs=(P("ctx", "fsdp", None, None), P(("ctx", "fsdp"), None)),
        check_vma=False,
    )
```

profile of v0, /device:TPU:0, one launch (start us, length us, event | category | flops | bytes accessed | tf_op | source)
XLA Modules:
  0.0 444.1 jit_solution(16017784369528222208)
XLA Ops:
  7.3 0.7 all-gather.11.cloned.1.call-update
  8.0 10.2 %all_gather.24 = bf16[256,1024]{1,0:T(8,128)(2,1)} all-gather(bf16[256,256]{1,0:T(8,128)(2,1)} %param.16), channel_id=1, replica_groups=mesh['ctx'=4,'fsdp'=8] {'ctx'}, dimensions={1}, use_global_device_ids=true | all-gather | bytes 655360 | tf_op jit(solution)/shard_map/all_gather | solution.py:159
  18.3 10.8 %all_gather.29 = bf16[256,1024]{1,0:T(8,128)(2,1)} all-gather(bf16[256,256]{1,0:T(8,128)(2,1)} %param.17), channel_id=1, replica_groups=mesh['ctx'=4,'fsdp'=8] {'ctx'}, dimensions={1}, use_global_device_ids=true | all-gather | bytes 655360 | tf_op jit(solution)/shard_map/all_gather | solution.py:160
  29.1 2.7 all-gather.11.cloned.1.call-done
  32.4 0.6 reduce-window.11
  33.7 0.3 fusion.15
  34.0 0.3 multiply_cosine_fusion
  34.3 73.1 %all-gather.7.cloned.1.call-done = bf16[2048,1024]{1,0:T(8,128)(2,1)} async-done(((bf16[256,1024]{1,0:T(8,128)(2,1)}), bf16[2048,1024]{1,0:T(8,128)(2,1)}) %all-gather.7.cloned.1.call-update) | async-done | bytes 4194320 | tf_op jit(solution)/shard_map/all_gather | solution.py:166
  107.4 6.5 %copy.60 = bf16[1024,2048]{1,0:T(8,128)(2,1)} copy(bf16[1024,2048]{0,1:T(8,128)(2,1)} %bitcast.130) | data formatting | bytes 8388608 | tf_op jit(solution)/shard_map/dot_general | solution.py:109
  113.9 3.9 multiply_reduce_fusion.1
  118.2 1.0 copy.61
  119.3 1.6 scatter_custom_fusion
  120.8 0.7 all_to_all.9
  121.5 2.6 all-to-all-start
  124.1 57.4 %all-gather.15.cloned.1.call-done = bf16[2048,1024]{1,0:T(8,128)(2,1)} async-done(((bf16[256,1024]{1,0:T(8,128)(2,1)}), bf16[2048,1024]{1,0:T(8,128)(2,1)}) %all-gather.15.cloned.1.call-update) | async-done | bytes 4194320 | tf_op jit(solution)/shard_map/all_gather | solution.py:167
  181.5 3.5 convolution_convert_fusion
  185.0 3.7 scatter_custom_fusion.1
  188.8 2.9 all-to-all-start.1
  191.6 0.2 all-gather.17.cloned.1.call-start
  191.9 0.3 all-gather.17.cloned.1.call-update
  192.5 0.5 broadcast.432
  193.0 0.7 reduce.7
  193.8 81.3 %all-to-all-done.1 = bf16[32,16,2048]{2,1,0:T(8,128)(2,1)S(1)} async-done(((bf16[32,16,2048]{2,1,0:T(8,128)(2,1)}), bf16[32,16,2048]{2,1,0:T(8,128)(2,1)S(1)}, u32[]{:S(2)}, u32[]{:S(2)}) %all-to-all-start.1) | async-done | bytes 2097184 | tf_op jit(solution)/shard_map/all_to_all | solution.py:211
  275.1 5.1 %scatter_custom_fusion.2 = bf16[512,2048]{1,0:T(8,128)(2,1)} fusion(s32[512]{0:T(512)S(1)} %bitcast.142, bf16[512,2048]{1,0:T(8,128)(2,1)S(1)} %bitcast.133, bf16[]{:T(256)} %constant.125.clone.1), kind=kCustom, calls=%fused_computation.44 | custom fusion | bytes 2097154 | tf_op jit(solution)/shard_map/scatter | solution.py:229
  280.2 65.6 %all-gather.13.cloned.1.call-done = bf16[2048,2048]{1,0:T(8,128)(2,1)} async-done(((bf16[256,2048]{1,0:T(8,128)(2,1)}), bf16[2048,2048]{1,0:T(8,128)(2,1)}) %all-gather.13.cloned.1.call-update) | async-done | bytes 8388624 | tf_op jit(solution)/shard_map/all_gather | solution.py:165
  345.8 12.5 %copy.62 = bf16[2048,2048]{1,0:T(8,128)(2,1)} copy(bf16[2048,2048]{0,1:T(8,128)(2,1)} %bitcast.127) | data formatting | bytes 16777216 | tf_op jit(solution)/shard_map/dot_general | solution.py:109
  358.3 5.9 %multiply_reduce_fusion = (f32[256,16]{0,1:T(8,128)S(1)}, f32[256,16,128]{0,2,1:T(8,128)S(1)}) fusion(bf16[16,128,2048]{2,1,0:T(8,128)(2,1)} %bitcast.128, bf16[1,1,256,2048]{3,2,1,0:T(8,128)(2,1)S(1)} %copy-done.3, f32[2048]{0:T(1024)S(1)} %copy-done.9, f32[256]{0:T(256)S(1)} %add_rsqrt_fusion.2), kind=kOutput, calls=%fused_computation.36 | convolution fusion | flops 2150625280 | bytes 11559936 | tf_op jit(solution)/shard_map/dot_general | solution.py:109
  364.3 0.4 multiply_multiply_fusion
  364.6 0.3 subtract_convert_fusion
  365.1 1.3 copy.64
  366.4 1.7 all-gather.9.cloned.1.call-done
  368.0 24.0 %all-gather.17.cloned.1.call-done = bf16[1024,1024]{1,0:T(8,128)(2,1)} async-done(((bf16[256,1024]{1,0:T(8,128)(2,1)}), bf16[1024,1024]{1,0:T(8,128)(2,1)}) %all-gather.17.cloned.1.call-update) | async-done | bytes 2097168 | tf_op jit(solution)/shard_map/all_gather | solution.py:180
  392.1 41.9 %while.15 = (s32[]{:T(128)}, f32[256,8,2]{0,2,1:T(2,128)S(1)}, f32[256,8,2]{0,2,1:T(2,128)S(1)}, f32[256,8,2,128]{0,3,2,1:T(8,128)}, s32[256]{0:T(256)S(1)}, /*i...) while((s32[]{:T(128)}, f32[256,8,2]{0,2,1:T(2,128)S(1)}, ...), condition=%wide.region_12.13_spmd.clone, body=%wide.region_9.12_spmd.clone.sunk | while | flops 1102991360 | bytes 41695372 | solution.py:86
  392.1 0.2 compare_and_fusion.2
  392.3 1.7 constant_dynamic-slice_fusion.8
  394.0 0.5 copy.83
  394.6 6.0 %fusion.71 = (f32[256,8,2]{0,2,1:T(2,128)S(1)}, f32[8,512,256,2]{2,1,3,0:T(8,128)}) fusion(pred[256,512]{0,1:T(8,128)(4,1)S(1)} %compare_and_fusion.2, bf16[512,8,128,1]{0,2,3,1:T(8,128)(2,1)S(1)} %bitcast.123, bf16[256,8,2,128]{3,0,2,1:T(8,128)(2,1)} %get-tuple-element.315), kind=kOutput, calls=%fused_computation.5.clone.1 | convolution fusion | flops 543158272 | bytes 10633216 | tf_op jit(solution)/shard_map/while/body/eval_jaxpr/tkgd,skd->tkgs/dot_general | solution.py:44
  400.6 4.5 %fusion.73 = f32[256,8,2]{0,2,1:T(2,128)S(1)} fusion(f32[8,512,256,2]{2,1,3,0:T(8,128)} %get-tuple-element.276, f32[256,8,2]{0,2,1:T(2,128)S(1)} %fusion.72, pred[256,512]{0,1:T(8,128)(4,1)S(1)} %compare_and_fusion.2), kind=kLoop, calls=%fused_computation.7.clone.1 | loop fusion | flops 10481664 | bytes 8552448 | tf_op jit(solution)/shard_map/while/body/eval_jaxpr/reduce_sum | solution.py:54
  405.1 0.5 copy.84
  405.7 7.1 %bitcast_add_fusion.3 = f32[256,8,2,128]{0,3,2,1:T(8,128)} fusion(f32[256,8,2,128]{0,3,2,1:T(8,128)} %get-tuple-element.296, bf16[512,8,128,1]{0,2,3,1:T(8,128)(2,1)S(1)} %bitcast.124, f32[8,512,256,2]{2,1,3,0:T(8,128)} %get-tuple-element.276, f32[256,8,2]{0,2,1:T(2,128)S(1)} %fusion.72, pred[256,512]{0,1:T(8,128)(4,1)S(1)} %compare_and_fusion.2, ...), kind=kOutput, calls=%fused_computation.10.clone.1 | convolution fusion | flops 548929536 | bytes 13795329 | tf_op jit(solution)/shard_map/while/body/eval_jaxpr/tkgs,skd->tkgd/dot_general | solution.py:55
  413.0 1.7 constant_dynamic-slice_fusion.8
  414.7 0.5 copy.83
  415.2 6.0 %fusion.71 = (f32[256,8,2]{0,2,1:T(2,128)S(1)}, f32[8,512,256,2]{2,1,3,0:T(8,128)}) fusion(pred[256,512]{0,1:T(8,128)(4,1)S(1)} %compare_and_fusion.2, bf16[512,8,128,1]{0,2,3,1:T(8,128)(2,1)S(1)} %bitcast.123, bf16[256,8,2,128]{3,0,2,1:T(8,128)(2,1)} %get-tuple-element.315), kind=kOutput, calls=%fused_computation.5.clone.1 | convolution fusion | flops 543158272 | bytes 10633216 | tf_op jit(solution)/shard_map/while/body/eval_jaxpr/tkgd,skd->tkgs/dot_general | solution.py:44
  421.3 4.5 %fusion.73 = f32[256,8,2]{0,2,1:T(2,128)S(1)} fusion(f32[8,512,256,2]{2,1,3,0:T(8,128)} %get-tuple-element.276, f32[256,8,2]{0,2,1:T(2,128)S(1)} %fusion.72, pred[256,512]{0,1:T(8,128)(4,1)S(1)} %compare_and_fusion.2), kind=kLoop, calls=%fused_computation.7.clone.1 | loop fusion | flops 10481664 | bytes 8552448 | tf_op jit(solution)/shard_map/while/body/eval_jaxpr/reduce_sum | solution.py:54
  425.8 0.5 copy.84
  426.3 7.7 %bitcast_add_fusion.3 = f32[256,8,2,128]{0,3,2,1:T(8,128)} fusion(f32[256,8,2,128]{0,3,2,1:T(8,128)} %get-tuple-element.296, bf16[512,8,128,1]{0,2,3,1:T(8,128)(2,1)S(1)} %bitcast.124, f32[8,512,256,2]{2,1,3,0:T(8,128)} %get-tuple-element.276, f32[256,8,2]{0,2,1:T(2,128)S(1)} %fusion.72, pred[256,512]{0,1:T(8,128)(4,1)S(1)} %compare_and_fusion.2, ...), kind=kOutput, calls=%fused_computation.10.clone.1 | convolution fusion | flops 548929536 | bytes 13795329 | tf_op jit(solution)/shard_map/while/body/eval_jaxpr/tkgs,skd->tkgd/dot_general | solution.py:55
  434.0 1.8 divide_convert_fusion
  435.8 1.4 copy.73
  (75 shorter events, 2.5 us)
Async XLA Ops:
  7.2 24.8 %copy-start.6 = (s32[8,4]{0,1:T(4,128)S(1)}, s32[8,4]{0,1:T(4,128)}, u32[]{:S(2)}) copy-start(s32[8,4]{0,1:T(4,128)} %param.20) | copy-start | bytes 388
  7.2 24.8 %copy-start.5 = (s32[8,4]{0,1:T(4,128)S(1)}, s32[8,4]{0,1:T(4,128)}, u32[]{:S(2)}) copy-start(s32[8,4]{0,1:T(4,128)} %param.21) | copy-start | bytes 388
  7.2 25.2 %copy-start.4 = (s32[1,1,256]{2,1,0:T(1,128)S(1)}, s32[1,1,256]{2,1,0:T(1,128)}, u32[]{:S(2)}) copy-start(s32[1,1,256]{2,1,0:T(1,128)} %param.22) | copy-start | bytes 3076
  7.2 26.5 %copy-start.2 = (bf16[1,1,256,2048]{3,2,1,0:T(8,128)(2,1)S(1)}, bf16[1,1,256,2048]{3,2,1,0:T(8,128)(2,1)}, u32[]{:S(2)}) copy-start(bf16[1,1,256,2048]{3,2,1,0:T(8,128)(2,1)} %param.13) | copy-start | bytes 3145732
  7.2 24.7 %all-gather.11.cloned.1.call-start = ((), (), s32[]{:S(2)}) async-start(), calls=%async_computation.4 | async-start | bytes 1310720 | tf_op jit(solution)/shard_map/all_gather | solution.py:158
  7.9 99.5 %all-gather.7.cloned.1.call-start = ((), (), s32[]{:S(2)}) async-start(), calls=%async_computation.2 | async-start | bytes 4718592 | tf_op jit(solution)/shard_map/all_gather | solution.py:166
  18.3 163.3 %all-gather.15.cloned.1.call-start = ((), (), s32[]{:S(2)}) async-start(), calls=%async_computation.6 | async-start | bytes 4718592 | tf_op jit(solution)/shard_map/all_gather | solution.py:167
  29.1 316.7 %all-gather.13.cloned.1.call-start = ((), (), s32[]{:S(2)}) async-start(), calls=%async_computation.5 | async-start | bytes 9437184 | tf_op jit(solution)/shard_map/all_gather | solution.py:165
  31.9 336.1 %all-gather.9.cloned.1.call-start = ((), (), s32[]{:S(2)}) async-start(), calls=%async_computation.3 | async-start | bytes 2621440 | tf_op jit(solution)/shard_map/all_gather | solution.py:179
  107.4 6.5 %copy-start.9 = (f32[2048]{0:T(1024)S(1)}, f32[2048]{0:T(1024)}, u32[]{:S(2)}) copy-start(f32[2048]{0:T(1024)} %param.14) | copy-start | bytes 24580
  113.9 3.9 copy-start.7
  121.5 67.2 %all-to-all-start = ((s32[32,1,16]{2,1,0:T(1,128)}), s32[32,1,16]{2,1,0:T(1,128)S(1)}, u32[]{:S(2)}, u32[]{:S(2)}) async-start(s32[32,1,16]{2,1,0:T(1,128)} %bitcast.24), calls=%async_computation | async-start | bytes 32768 | tf_op jit(solution)/shard_map/all_to_all | solution.py:218
  124.1 60.9 %copy-start = (bf16[256,1024]{1,0:T(8,128)(2,1)S(1)}, bf16[256,1024]{1,0:T(8,128)(2,1)}, u32[]{:S(2)}) copy-start(bf16[256,1024]{1,0:T(8,128)(2,1)} %copy.61) | copy-start | bytes 1572868
  185.0 3.7 copy-start.1
  188.8 86.4 %all-to-all-start.1 = ((bf16[32,16,2048]{2,1,0:T(8,128)(2,1)}), bf16[32,16,2048]{2,1,0:T(8,128)(2,1)S(1)}, u32[]{:S(2)}, u32[]{:S(2)}) async-start(bf16[32,16,2048]{2,1,0:T(8,128)(2,1)} %bitcast.26), calls=%async_computation.1 | async-start | bytes 4194304 | tf_op jit(solution)/shard_map/all_to_all | solution.py:211
  191.6 200.4 %all-gather.17.cloned.1.call-start = ((), (), s32[]{:S(2)}) async-start(), calls=%async_computation.7 | async-start | bytes 2621440 | tf_op jit(solution)/shard_map/all_gather | solution.py:180
  345.8 12.5 %copy-start.3 = (bf16[1,1,256,2048]{3,2,1,0:T(8,128)(2,1)S(1)}, bf16[1,1,256,2048]{3,2,1,0:T(8,128)(2,1)}, u32[]{:S(2)}) copy-start(bf16[1,1,256,2048]{3,2,1,0:T(8,128)(2,1)} %param.13) | copy-start | bytes 3145732
  358.3 6.0 %copy-start.8 = (f32[128]{0:T(128)S(1)}, f32[128]{0:T(128)}, u32[]{:S(2)}) copy-start(f32[128]{0:T(128)} %param.18) | copy-start | bytes 1540
Sparse Core Ops, SparseCore 0:
  9.6 22.2 all-gather.10
  34.0 73.3 all-gather.6
  109.6 71.9 all-gather.14
  183.5 162.2 all-gather.12
  347.2 20.7 all-gather.8
  369.5 22.5 all-gather.16
where the time goes:
time: 445 us; the launch traced here: 444 us
  waiting for transfers between devices  307 us (69%)
  matrix products  40 us (9%)
  local copies, waits for them, and re-layouts  36.8 us (8%)
  blocking collectives  21 us (5%)
  other arithmetic  18.9 us (4%)
  between operations  14.4 us (3%)
  starting transfers between devices  5.9 us (1%)
    all_to_all x1, waiting for transfers between devices, shards(): lax.all_to_all(bucket.reshape(owner_count, per_owner, kv_width), ('ctx',...  81.3 us
    all_gather x1, waiting for transfers between devices, shards(): lax.all_gather(key_cols, 'fsdp', axis=0, tiled=True)  73.1 us
    all_gather x1, waiting for transfers between devices, shards(): lax.all_gather(query_cols, 'fsdp', axis=0, tiled=True)  65.6 us
    all_gather x1, waiting for transfers between devices, shards(): lax.all_gather(value_cols, 'fsdp', axis=0, tiled=True)  57.4 us
    all_gather x1, waiting for transfers between devices, shards(): lax.all_gather(value_new, 'ctx', axis=0, tiled=True)  24 us
    dot_general x2, local copies, waits for them, and re-layouts, project_rows(): jnp.dot(source, shard_rows, preferred_element_type=jnp.float32)  19 us
    dot_general x2, matrix products, attend_keys(): jnp.einsum('tkgs,skd->tkgd', weights.astype(jnp.bfloat16), heads_of_value...  14.8 us
    dot_general x3, matrix products, project_rows(): jnp.dot(source, shard_rows, preferred_element_type=jnp.float32)  13.3 us
  transfers between devices with their start and end apart: 8, of which 7 were waited for; matrix products, arithmetic and copies ran while one was open for 11% of the time, Pallas kernels for 0%

commit v1 on v0

v1 whole, which is shorter than its diff:
```python
import functools
import math

import jax
import jax.numpy as jnp
from jax import lax
from jax.experimental import pallas as pl
from jax.experimental.pallas import tpu as pltpu
from jax.sharding import PartitionSpec as P

HEAD_WIDTH = 128
EPSILON = 1e-06
THETA = 1000000.0
NEG_BIG = -1e30
MESH = pl.DeviceIdType.MESH
LINE = 4
CORES = 2
BF = jnp.bfloat16
F32 = jnp.float32


def dot_nt(a, b):
    return lax.dot_general(a, b, (((1,), (1,)), ((), ())), preferred_element_type=F32)


def aligned(index, size):
    return pl.multiple_of(index * size, size)


def kernel(
    ctx_n, fsdp_n, seg_n,
    lengths, pieces, hidden, norm_gain, w_q, w_k, w_v, q_gain, k_gain, owner, slot,
    attended_out, cache_out,
    normed, wkv, wq, tab, cos_t, sin_t, kv, q_rows, bucket, got, slot2d, slot_msg, slot_got,
    attn, attn_got,
    w_send, w_recv, h_send, h_recv, f_send, t_send, t_recv,
    c_send, c_recv, s_send, s_recv, a_send, a_recv,
):
    ctx = lax.axis_index("ctx")
    fs = lax.axis_index("fsdp")
    me = ctx * fsdp_n + fs
    total_n = ctx_n * fsdp_n
    tok = hidden.shape[0]
    wide = w_q.shape[0]
    kc = w_k.shape[1]
    qc = w_q.shape[1]
    per = got.shape[1] // fsdp_n
    most = per // ctx_n
    minor_n = fsdp_n // LINE
    rows_y = ctx_n // CORES
    major, minor = fs // minor_n, fs % minor_n
    y_at, core = ctx // CORES, ctx % CORES
    sibling = y_at * CORES + (1 - core)

    barrier = pltpu.get_barrier_semaphore()

    @pl.loop(1, total_n)
    def _(step):
        other = (me + step) % total_n
        pl.semaphore_signal(
            barrier, inc=1, device_id=(other // fsdp_n, other % fsdp_n), device_id_type=MESH
        )

    wkv[pl.ds(aligned(fs, wide), wide), 0:kc] = w_k[...]
    wkv[pl.ds(aligned(fs, wide), wide), kc : 2 * kc] = w_v[...]
    wq[pl.ds(aligned(fs, wide), wide), :] = w_q[...]
    tab[ctx] = jnp.concatenate(
        [owner[...], slot[...], jnp.zeros((6, tok), jnp.int32)], axis=0
    )
    pl.semaphore_wait(barrier, total_n - 1)

    buffers = (wkv, wq)

    def w_copy(part, target, shard):
        spot = buffers[part].at[pl.ds(aligned(shard, wide), wide), :]
        to = ((fs + minor_n) % fsdp_n, (fs + fsdp_n - minor_n) % fsdp_n)[target] if target < 2 else (
            major * minor_n + (minor + target - 1) % minor_n
        )
        return pltpu.make_async_remote_copy(
            src_ref=spot, dst_ref=spot,
            send_sem=w_send.at[part, target, shard], recv_sem=w_recv.at[part, shard],
            device_id=(ctx, to), device_id_type=MESH,
        )

    def w_minors(part, shard):
        for target in range(2, minor_n + 1):
            w_copy(part, target, shard).start()

    def w_own(part):
        @pl.when(major < LINE - 1)
        def _():
            w_copy(part, 0, fs).start()

        @pl.when(major > 0)
        def _():
            w_copy(part, 1, fs).start()

        w_minors(part, fs)

    def w_step(part, k):
        @pl.when(major - k >= 0)
        def _():
            shard = fs - k * minor_n
            w_copy(part, 0, shard).wait_recv()

            @pl.when(major < LINE - 1)
            def _():
                w_copy(part, 0, shard).start()

            w_minors(part, shard)

        @pl.when(major + k < LINE)
        def _():
            shard = fs + k * minor_n
            w_copy(part, 1, shard).wait_recv()

            @pl.when(major > 0)
            def _():
                w_copy(part, 1, shard).start()

            w_minors(part, shard)

    def w_finish(part):
        for step in range(1, minor_n):
            for line in range(LINE):
                w_copy(part, 0, line * minor_n + (minor + step) % minor_n).wait_recv()

    def w_sent(part):
        for line in range(LINE):
            shard = line * minor_n + minor

            @pl.when((major < LINE - 1) & (line <= major))
            def _():
                w_copy(part, 0, shard).wait_send()

            @pl.when((major > 0) & (line >= major))
            def _():
                w_copy(part, 1, shard).wait_send()

            for target in range(2, minor_n + 1):
                w_copy(part, target, shard).wait_send()

    def h_copy(block, to, send_sem):
        spot = normed.at[pl.ds(aligned(block, tok), tok), :]
        return pltpu.make_async_remote_copy(
            src_ref=spot, dst_ref=spot, send_sem=send_sem, recv_sem=h_recv.at[block],
            device_id=(to, fs), device_id_type=MESH,
        )

    def t_copy(block, to):
        return pltpu.make_async_remote_copy(
            src_ref=tab.at[block], dst_ref=tab.at[block],
            send_sem=t_send.at[to], recv_sem=t_recv.at[block],
            device_id=(to, fs), device_id_type=MESH,
        )

    def across(step):
        return ((y_at + step) % rows_y) * CORES + core

    w_own(0)
    inputs = hidden[...].astype(F32)
    factor = lax.rsqrt(jnp.mean(inputs * inputs, axis=-1, keepdims=True) + EPSILON)
    normed[pl.ds(aligned(ctx, tok), tok), :] = (inputs * factor * norm_gain[...]).astype(BF)
    for step in range(1, rows_y):
        h_copy(ctx, across(step), h_send.at[step]).start()
    h_copy(ctx, sibling, h_send.at[0]).start()
    w_own(1)
    for step in range(1, ctx_n):
        t_copy(ctx, (ctx + step) % ctx_n).start()

    ends = []
    running = jnp.int32(0)
    for j in range(seg_n):
        running = running + lengths[fs, j]
        ends.append(running)

    def first_place(pos):
        first = jnp.zeros_like(pos)
        for end in ends:
            first = jnp.where(pos >= end, end, first)
        return first

    lane = lax.broadcasted_iota(jnp.int32, (1, HEAD_WIDTH), 1)
    half = HEAD_WIDTH // 2
    frequency = jnp.exp(
        (lane % half).astype(F32) * (-2.0 * math.log(THETA) / HEAD_WIDTH)
    )

    @pl.loop(0, ctx_n)
    def _(c):
        pos = lax.broadcasted_iota(jnp.int32, (tok, HEAD_WIDTH), 0) + pieces[fs, c] * tok
        angles = (pos - first_place(pos)).astype(F32) * frequency
        sine = jnp.sin(angles)
        at = pl.ds(aligned(c, tok), tok)
        cos_t[at, :] = jnp.cos(angles)
        sin_t[at, :] = jnp.where(lane < half, -sine, sine)

    for k in range(1, LINE):
        w_step(0, k)
        w_step(1, k)
        if k == 1:
            for step in range(1, rows_y):
                block = across(step)
                h_copy(block, sibling, h_send.at[0]).wait_recv()
                h_copy(block, sibling, f_send.at[block]).start()
    for step in range(1, ctx_n):
        t_copy((ctx + step) % ctx_n, ctx).wait_recv()

    owners = lax.broadcasted_iota(jnp.int32, (total_n, tok), 0)
    before = jnp.where(
        lax.broadcasted_iota(jnp.int32, (tok, tok), 0)
        < lax.broadcasted_iota(jnp.int32, (tok, tok), 1),
        1.0, 0.0,
    ).astype(BF)
    lane_shift = (fs * per) % HEAD_WIDTH
    places = []
    slots = jnp.zeros((total_n, HEAD_WIDTH), F32)
    for c in range(ctx_n):
        owner_row = tab[c, 0:1, :]
        slot_row = tab[c, 1:2, :] + 1
        mine = jnp.where(owners == owner_row, 1.0, 0.0)
        earlier = jnp.dot(mine.astype(BF), before, preferred_element_type=F32)
        rank = jnp.sum(mine * earlier, axis=0, keepdims=True).astype(jnp.int32)
        places.append(owner_row * per + c * most + rank)
        column = rank + (c * most + lane_shift)
        spread = jnp.where(
            lax.broadcasted_iota(jnp.int32, (HEAD_WIDTH, tok), 0) == column, 1.0, 0.0
        ).astype(BF)
        high = (mine * (slot_row // 32).astype(F32)).astype(BF)
        low = (mine * (slot_row % 32).astype(F32)).astype(BF)
        slots = slots + dot_nt(high, spread) * 32.0 + dot_nt(low, spread)
    place_row = jnp.concatenate(places, axis=1)
    slot2d[...] = slots

    @pl.loop(0, total_n)
    def _(o):
        slot_msg[o] = jnp.broadcast_to(slot2d[pl.ds(o, 1), :], (8, HEAD_WIDTH))

    w_finish(0)
    h_copy(sibling, sibling, h_send.at[0]).wait_recv()
    for step in range(1, rows_y):
        h_copy(((y_at + step) % rows_y) * CORES + 1 - core, sibling, h_send.at[0]).wait_recv()

    def norm_rope(x, gain, cosine, sine):
        scale = lax.rsqrt(jnp.mean(x * x, axis=-1, keepdims=True) + EPSILON)
        y = x * scale * gain
        return (y * cosine + pltpu.roll(y, half, 1) * sine).astype(BF)

    @pl.loop(0, ctx_n)
    def _(c):
        at = pl.ds(aligned(c, tok), tok)
        raw = jnp.dot(normed[at, :], wkv[...], preferred_element_type=F32)
        cosine, sine = cos_t[at, :], sin_t[at, :]
        for h in range(kc // HEAD_WIDTH):
            cols = slice(h * HEAD_WIDTH, (h + 1) * HEAD_WIDTH)
            kv[at, cols] = norm_rope(raw[:, cols], k_gain[...], cosine, sine)
        kv[at, kc : 2 * kc] = raw[:, kc:].astype(BF)

    chunk = 256

    @pl.loop(0, total_n * per // chunk)
    def _(i):
        rows = lax.broadcasted_iota(jnp.int32, (chunk, ctx_n * tok), 0) + i * chunk
        pick = jnp.where(rows == place_row, 1.0, 0.0).astype(BF)
        bucket[pl.ds(aligned(i, chunk), chunk), :] = jnp.dot(
            pick, kv[...], preferred_element_type=F32
        ).astype(BF)

    def c_copy(to, sender):
        return pltpu.make_async_remote_copy(
            src_ref=bucket.at[pl.ds(aligned(to, per), per), :],
            dst_ref=got.at[sender // fsdp_n, pl.ds(aligned(sender % fsdp_n, per), per), :],
            send_sem=c_send.at[to], recv_sem=c_recv.at[sender],
            device_id=(to // fsdp_n, to % fsdp_n), device_id_type=MESH,
        )

    def s_copy(to, sender):
        return pltpu.make_async_remote_copy(
            src_ref=slot_msg.at[to], dst_ref=slot_got.at[sender],
            send_sem=s_send.at[to], recv_sem=s_recv.at[sender],
            device_id=(to // fsdp_n, to % fsdp_n), device_id_type=MESH,
        )

    @pl.loop(1, total_n)
    def _(step):
        to = (me + step) % total_n
        c_copy(to, me).start()

        @pl.when(ctx == 0)
        def _():
            s_copy(to, fs).start()

    got[ctx, pl.ds(aligned(fs, per), per), :] = bucket[pl.ds(aligned(me, per), per), :]

    @pl.when(ctx == 0)
    def _():
        slot_got[fs] = slot_msg[me]

    w_finish(1)

    @pl.loop(0, ctx_n)
    def _(c):
        at = pl.ds(aligned(c, tok), tok)
        raw = jnp.dot(normed[at, :], wq[...], preferred_element_type=F32)
        cosine, sine = cos_t[at, :], sin_t[at, :]
        for h in range(qc // HEAD_WIDTH):
            cols = slice(h * HEAD_WIDTH, (h + 1) * HEAD_WIDTH)
            q_rows[at, cols] = norm_rope(raw[:, cols], q_gain[...], cosine, sine)

    key_pos = jnp.concatenate(
        [
            lax.broadcasted_iota(jnp.int32, (1, tok), 1) + pieces[fs, c] * tok
            for c in range(ctx_n)
        ],
        axis=1,
    )

    def a_copy(block, sender):
        return pltpu.make_async_remote_copy(
            src_ref=attn.at[pl.ds(aligned(block, tok), tok), :], dst_ref=attn_got.at[sender],
            send_sem=a_send.at[block], recv_sem=a_recv.at[sender],
            device_id=(block, fs), device_id_type=MESH,
        )

    group_width = qc // kc

    @pl.loop(0, ctx_n)
    def _(step):
        c = (ctx + 1 + step) % ctx_n
        at = pl.ds(aligned(c, tok), tok)
        pos = lax.broadcasted_iota(jnp.int32, (tok, 1), 0) + pieces[fs, c] * tok
        visible = (key_pos <= pos) & (key_pos >= first_place(pos))
        for h in range(qc // HEAD_WIDTH):
            j = h // group_width
            cols = slice(h * HEAD_WIDTH, (h + 1) * HEAD_WIDTH)
            keys = kv[:, j * HEAD_WIDTH : (j + 1) * HEAD_WIDTH]
            values = kv[:, kc + j * HEAD_WIDTH : kc + (j + 1) * HEAD_WIDTH]
            scores = dot_nt(q_rows[at, cols], keys) * (1.0 / math.sqrt(HEAD_WIDTH))
            masked = jnp.where(visible, scores, NEG_BIG)
            weights = jnp.exp(masked - jnp.max(masked, axis=-1, keepdims=True))
            total = jnp.sum(weights, axis=-1, keepdims=True)
            mixed = jnp.dot(weights.astype(BF), values, preferred_element_type=F32)
            attn[at, cols] = (mixed / total).astype(BF)

        @pl.when(step < ctx_n - 1)
        def _():
            a_copy(c, ctx).start()

    attn_got[ctx] = attn[pl.ds(aligned(ctx, tok), tok), :]

    for g in range(fsdp_n):
        @pl.when((ctx > 0) | (fs != g))
        def _():
            s_copy(me, g).wait_recv()

    shared = HEAD_WIDTH // per
    slot_line = jnp.concatenate(
        [
            sum(slot_got[p * shared + i, 0:1, :] for i in range(shared))
            for p in range(fsdp_n // shared)
        ],
        axis=1,
    )
    cap = cache_out.shape[0]
    place = jnp.where(
        lax.broadcasted_iota(jnp.int32, (cap, fsdp_n * per), 0) + 1
        == slot_line.astype(jnp.int32),
        1.0, 0.0,
    ).astype(BF)

    for step in range(1, ctx_n):
        a_copy(ctx, (ctx + step) % ctx_n).wait_recv()
    for c in range(ctx_n):
        attended_out[:, c * qc : (c + 1) * qc] = attn_got[c]

    @pl.loop(1, total_n)
    def _(step):
        c_copy(me, (me + step) % total_n).wait_recv()

    for c in range(ctx_n):
        rows = jnp.dot(place, got[c], preferred_element_type=F32).astype(BF)
        cache_out[:, c * kc : (c + 1) * kc] = rows[:, :kc]
        cache_out[:, (ctx_n + c) * kc : (ctx_n + c + 1) * kc] = rows[:, kc:]

    w_sent(0)
    w_sent(1)
    for step in range(1, rows_y):
        h_copy(ctx, across(step), h_send.at[step]).wait_send()
        block = across(step)
        h_copy(block, sibling, f_send.at[block]).wait_send()
    h_copy(ctx, sibling, h_send.at[0]).wait_send()
    for step in range(1, ctx_n):
        t_copy(ctx, (ctx + step) % ctx_n).wait_send()
        a_copy((ctx + step) % ctx_n, ctx).wait_send()

    @pl.loop(1, total_n)
    def _(step):
        to = (me + step) % total_n
        c_copy(to, me).wait_send()

        @pl.when(ctx == 0)
        def _():
            s_copy(to, fs).wait_send()


def shards(
    ctx_n, fsdp_n,
    hidden, norm_gain, w_query, w_key, w_value, q_gain, k_gain, lengths, piece_map, owner, slot,
):
    tok, width = hidden.shape[2:]
    kc, qc = w_key.shape[1], w_query.shape[1]
    total_n = ctx_n * fsdp_n
    most = 2 * tok // total_n
    per = ctx_n * most
    stream = ctx_n * tok
    minor_n = fsdp_n // LINE
    vmem = pl.BlockSpec(memory_space=pltpu.VMEM)
    smem = pl.BlockSpec(memory_space=pltpu.SMEM)
    dma = pltpu.SemaphoreType.DMA
    attended, cache = pl.pallas_call(
        functools.partial(kernel, ctx_n, fsdp_n, lengths.shape[1]),
        out_shape=(
            jax.ShapeDtypeStruct((tok, ctx_n * qc), BF),
            jax.ShapeDtypeStruct((total_n * most, 2 * ctx_n * kc), BF),
        ),
        in_specs=[smem, smem] + [vmem] * 9,
        out_specs=(vmem, vmem),
        scratch_shapes=[
            pltpu.VMEM((stream, width), BF),
            pltpu.VMEM((width, 2 * kc), BF),
            pltpu.VMEM((width, qc), BF),
            pltpu.VMEM((ctx_n, 8, tok), jnp.int32),
            pltpu.VMEM((stream, HEAD_WIDTH), F32),
            pltpu.VMEM((stream, HEAD_WIDTH), F32),
            pltpu.VMEM((stream, 2 * kc), BF),
            pltpu.VMEM((stream, qc), BF),
            pltpu.VMEM((total_n * per, 2 * kc), BF),
            pltpu.VMEM((ctx_n, fsdp_n * per, 2 * kc), BF),
            pltpu.VMEM((total_n, HEAD_WIDTH), F32),
            pltpu.VMEM((total_n, 8, HEAD_WIDTH), F32),
            pltpu.VMEM((fsdp_n, 8, HEAD_WIDTH), F32),
            pltpu.VMEM((stream, qc), BF),
            pltpu.VMEM((ctx_n, tok, qc), BF),
            dma((2, minor_n + 1, fsdp_n)),
            dma((2, fsdp_n)),
            dma((ctx_n,)),
            dma((ctx_n,)),
            dma((ctx_n,)),
            dma((ctx_n,)),
            dma((ctx_n,)),
            dma((total_n,)),
            dma((total_n,)),
            dma((total_n,)),
            dma((fsdp_n,)),
            dma((ctx_n,)),
            dma((ctx_n,)),
        ],
        compiler_params=pltpu.CompilerParams(
            collective_id=0, has_side_effects=True, vmem_limit_bytes=56 * 1024 * 1024
        ),
        name="prefill",
    )(
        lengths, piece_map, hidden[0, 0], norm_gain[None], w_query, w_key, w_value,
        q_gain[None], k_gain[None], owner[0], slot[0],
    )
    return (attended[None, None], cache)


def solution(mesh):
    placed = (
        P("ctx", "fsdp", None, None),
        P(),
        P("fsdp", "ctx"),
        P("fsdp", "ctx"),
        P("fsdp", "ctx"),
        P(),
        P(),
        P(),
        P(),
        P("ctx", "fsdp", None),
        P("ctx", "fsdp", None),
    )
    return jax.shard_map(
        functools.partial(shards, mesh.shape["ctx"], mesh.shape["fsdp"]),
        mesh=mesh,
        in_specs=placed,
        out_specs=(P("ctx", "fsdp", None, None), P(("ctx", "fsdp"), None)),
        check_vma=False,
    )
```

time: 445 us -> 115 us (0.26)
  waiting for transfers between devices: 307 us -> 0 us
  Pallas kernels: 0 us -> 107 us
  matrix products: 40 us -> 0 us
  local copies, waits for them, and re-layouts: 36.8 us -> 6.47 us
  blocking collectives: 21 us -> 0 us
  other arithmetic: 18.9 us -> 0 us
  between operations: 14.4 us -> 0.65 us
  starting transfers between devices: 5.9 us -> 0 us
    all_gather x6 -> x0, waiting for transfers between devices: 225 us -> none  [the longest x1 73.1 us: shards(): lax.all_gather(key_cols, 'fsdp', axis=0, tiled=True)]
    pallas_call x0 -> x1, Pallas kernels: none -> 107 us  [shards(): pl.pallas_call(functools.partial(kernel, ctx_n, fsdp_n, lengths.shape[1])...]
    all_to_all x2 -> x0, waiting for transfers between devices: 81.3 us -> none  [the longest x1 81.3 us: shards(): lax.all_to_all(bucket.reshape(owner_count, per_owner, kv_width), ('ctx',...]
    dot_general x7 -> x0, matrix products: 40 us -> none  [the longest x2 14.8 us: attend_keys(): jnp.einsum('tkgs,skd->tkgd', weights.astype(jnp.bfloat16), heads_of_value...]
    all_gather x2 -> x0, blocking collectives: 21 us -> none  [the longest x1 10.8 us: shards(): lax.all_gather(w_value, 'ctx', axis=1, tiled=True)]
    dot_general x2 -> x0, local copies, waits for them, and re-layouts: 19 us -> none  [project_rows(): jnp.dot(source, shard_rows, preferred_element_type=jnp.float32)]
    reduce_sum x9 -> x0, other arithmetic: 9.74 us -> none  [the longest x2 8.94 us: attend_keys(): row_sum = row_sum * shrink + jnp.sum(weights, axis=-1)]
    scatter x2 -> x0, local copies, waits for them, and re-layouts: 6.65 us -> none  [the longest x1 5.1 us: shards(): new_cache = jnp.zeros((capacity, kv_width), jnp.bfloat16).at[got_slots.re...]
  transfers between devices with their start and end apart: 8 -> 0, of which waited for: 7 -> 0; matrix products, arithmetic and copies ran while one was open for 11% -> 0% of each run, Pallas kernels for 0% -> 0%
where the time goes in v1:
time: 115 us
  Pallas kernels  107 us (93%)
  local copies, waits for them, and re-layouts  6.47 us (6%)
    pallas_call x1, Pallas kernels, shards(): pl.pallas_call(functools.partial(kernel, ctx_n, fsdp_n, lengths.shape[1])...  107 us
    unnamed x6, local copies, waits for them, and re-layouts  6.47 us

profile of v1, /device:TPU:0, one launch (start us, length us, event | category | flops | bytes accessed | tf_op | source)
XLA Modules:
  0.0 114.6 jit_solution(14256287544028955696)
XLA Ops:
  0.6 1.3 %copy.13.lengths = s32[8,4]{1,0:T(8,128)} copy(s32[8,4]{0,1:T(4,128)} %param.18) | data formatting | bytes 256 | tf_op args[7]
  2.0 1.3 %copy.14.pieces = s32[8,4]{1,0:T(8,128)} copy(s32[8,4]{0,1:T(4,128)} %param.19) | data formatting | bytes 256 | tf_op args[8]
  3.3 107.4 %prefill.1 = (bf16[256,2048]{1,0:T(8,128)(2,1)}, bf16[512,2048]{1,0:T(8,128)(2,1)}) custom-call(s32[8,4]{1,0:T(8,128)} %copy.13.lengths, s32[8,4]{1,0:T(8,128)} %copy.14.pieces, bf16[256,2048]{1,0:T(8,128)(2,1)} %bitcast.7, f32[1,2048]{1,0:T(1,128)} %bitcast.9, bf16[256,512]{1,0:T(8,128)(2,1)} %w_q.1, bf16[256,256]{1,0:T(8,128)(2,1)} %w_k.1, ...), custom_call_target="tpu_custom_call" | custom-call | tf_op jit(solution)/shard_map/prefill/pallas_call | solution.py:420
  110.8 0.0 copy-start
  110.8 2.5 %copy.17 = bf16[1,1,256,2048]{3,2,1,0:T(8,128)(2,1)} copy(bf16[1,1,256,2048]{3,2,1,0:T(8,128)(2,1)} %bitcast.8) | data formatting | bytes 2097152
  113.2 0.0 copy-done
  113.2 1.3 %copy.18 = bf16[512,2048]{1,0:T(8,128)(2,1)} copy(bf16[512,2048]{1,0:T(8,128)(2,1)S(1)} %copy-done) | data formatting | bytes 4194304
Async XLA Ops:
  110.8 2.5 %copy-start = (bf16[512,2048]{1,0:T(8,128)(2,1)S(1)}, bf16[512,2048]{1,0:T(8,128)(2,1)}, u32[]{:S(2)}) copy-start(bf16[512,2048]{1,0:T(8,128)(2,1)} %get-tuple-element.9) | copy-start | bytes 6291460

commit v2 on v1

--- a/solution.py
+++ b/solution.py
@@ -30,11 +30,11 @@
 def kernel(
     ctx_n, fsdp_n, seg_n,
     lengths, pieces, hidden, norm_gain, w_q, w_k, w_v, q_gain, k_gain, owner, slot,
-    attended_out, cache_out,
+    attn_out, got_out, line_out,
     normed, wkv, wq, tab, cos_t, sin_t, kv, q_rows, bucket, got, slot2d, slot_msg, slot_got,
     attn, attn_got,
     w_send, w_recv, h_send, h_recv, f_send, t_send, t_recv,
-    c_send, c_recv, s_send, s_recv, a_send, a_recv,
+    c_send, c_recv, s_send, s_recv, a_send, a_recv, o_sem,
 ):
     ctx = lax.axis_index("ctx")
     fs = lax.axis_index("fsdp")
@@ -164,14 +164,20 @@
     for step in range(1, rows_y):
         h_copy(ctx, across(step), h_send.at[step]).start()
     h_copy(ctx, sibling, h_send.at[0]).start()
-    w_own(1)
     for step in range(1, ctx_n):
         t_copy(ctx, (ctx + step) % ctx_n).start()
 
+    def entry(table, column):
+        at = (lax.broadcasted_iota(jnp.int32, table.shape, 0) == column) & (
+            lax.broadcasted_iota(jnp.int32, table.shape, 1) == fs
+        )
+        row = jnp.sum(jnp.where(at, table[...].astype(F32), 0.0), axis=0, keepdims=True)
+        return jnp.sum(row, axis=1, keepdims=True).astype(jnp.int32)
+
     ends = []
-    running = jnp.int32(0)
+    running = jnp.zeros((1, 1), jnp.int32)
     for j in range(seg_n):
-        running = running + lengths[fs, j]
+        running = running + entry(lengths, j)
         ends.append(running)
 
     def first_place(pos):
@@ -186,23 +192,23 @@
         (lane % half).astype(F32) * (-2.0 * math.log(THETA) / HEAD_WIDTH)
     )
 
-    @pl.loop(0, ctx_n)
-    def _(c):
-        pos = lax.broadcasted_iota(jnp.int32, (tok, HEAD_WIDTH), 0) + pieces[fs, c] * tok
-        angles = (pos - first_place(pos)).astype(F32) * frequency
-        sine = jnp.sin(angles)
-        at = pl.ds(aligned(c, tok), tok)
-        cos_t[at, :] = jnp.cos(angles)
-        sin_t[at, :] = jnp.where(lane < half, -sine, sine)
-
-    for k in range(1, LINE):
-        w_step(0, k)
-        w_step(1, k)
-        if k == 1:
-            for step in range(1, rows_y):
-                block = across(step)
-                h_copy(block, sibling, h_send.at[0]).wait_recv()
-                h_copy(block, sibling, f_send.at[block]).start()
+    def rope_tables(first, last):
+        @pl.loop(first, last)
+        def _(c):
+            pos = lax.broadcasted_iota(jnp.int32, (tok, HEAD_WIDTH), 0) + entry(pieces, c) * tok
+            angles = (pos - first_place(pos)).astype(F32) * frequency
+            sine = jnp.sin(angles)
+            at = pl.ds(aligned(c, tok), tok)
+            cos_t[at, :] = jnp.cos(angles)
+            sin_t[at, :] = jnp.where(lane < half, -sine, sine)
+
+    w_step(0, 1)
+    w_own(1)
+    rope_tables(0, ctx_n // 2)
+    w_step(0, 2)
+    rope_tables(ctx_n // 2, ctx_n)
+    w_step(0, 3)
+    w_step(1, 1)
     for step in range(1, ctx_n):
         t_copy((ctx + step) % ctx_n, ctx).wait_recv()
 
@@ -236,6 +242,11 @@
     def _(o):
         slot_msg[o] = jnp.broadcast_to(slot2d[pl.ds(o, 1), :], (8, HEAD_WIDTH))
 
+    for step in range(1, rows_y):
+        block = across(step)
+        h_copy(block, sibling, h_send.at[0]).wait_recv()
+        h_copy(block, sibling, f_send.at[block]).start()
+    w_step(1, 2)
     w_finish(0)
     h_copy(sibling, sibling, h_send.at[0]).wait_recv()
     for step in range(1, rows_y):
@@ -256,16 +267,6 @@
             kv[at, cols] = norm_rope(raw[:, cols], k_gain[...], cosine, sine)
         kv[at, kc : 2 * kc] = raw[:, kc:].astype(BF)
 
-    chunk = 256
-
-    @pl.loop(0, total_n * per // chunk)
-    def _(i):
-        rows = lax.broadcasted_iota(jnp.int32, (chunk, ctx_n * tok), 0) + i * chunk
-        pick = jnp.where(rows == place_row, 1.0, 0.0).astype(BF)
-        bucket[pl.ds(aligned(i, chunk), chunk), :] = jnp.dot(
-            pick, kv[...], preferred_element_type=F32
-        ).astype(BF)
-
     def c_copy(to, sender):
         return pltpu.make_async_remote_copy(
             src_ref=bucket.at[pl.ds(aligned(to, per), per), :],
@@ -281,14 +282,30 @@
             device_id=(to // fsdp_n, to % fsdp_n), device_id_type=MESH,
         )
 
-    @pl.loop(1, total_n)
+    chunk = 256
+    chunks = total_n * per // chunk
+    reach = chunk // per
+
+    @pl.loop(0, chunks)
     def _(step):
-        to = (me + step) % total_n
-        c_copy(to, me).start()
-
-        @pl.when(ctx == 0)
-        def _():
-            s_copy(to, fs).start()
+        i = (me // reach + 1 + 2 * (step % (chunks // 2)) + step // (chunks // 2)) % chunks
+        rows = lax.broadcasted_iota(jnp.int32, (chunk, ctx_n * tok), 0) + i * chunk
+        pick = jnp.where(rows == place_row, 1.0, 0.0).astype(BF)
+        bucket[pl.ds(aligned(i, chunk), chunk), :] = jnp.dot(
+            pick, kv[...], preferred_element_type=F32
+        ).astype(BF)
+
+        @pl.loop(0, reach)
+        def _(inner):
+            to = i * reach + (me + inner) % reach
+
+            @pl.when(to != me)
+            def _():
+                c_copy(to, me).start()
+
+                @pl.when(ctx == 0)
+                def _():
+                    s_copy(to, fs).start()
 
     got[ctx, pl.ds(aligned(fs, per), per), :] = bucket[pl.ds(aligned(me, per), per), :]
 
@@ -296,6 +313,7 @@
     def _():
         slot_got[fs] = slot_msg[me]
 
+    w_step(1, 3)
     w_finish(1)
 
     @pl.loop(0, ctx_n)
@@ -309,7 +327,7 @@
 
     key_pos = jnp.concatenate(
         [
-            lax.broadcasted_iota(jnp.int32, (1, tok), 1) + pieces[fs, c] * tok
+            lax.broadcasted_iota(jnp.int32, (1, tok), 1) + entry(pieces, c) * tok
             for c in range(ctx_n)
         ],
         axis=1,
@@ -328,7 +346,7 @@
     def _(step):
         c = (ctx + 1 + step) % ctx_n
         at = pl.ds(aligned(c, tok), tok)
-        pos = lax.broadcasted_iota(jnp.int32, (tok, 1), 0) + pieces[fs, c] * tok
+        pos = lax.broadcasted_iota(jnp.int32, (tok, 1), 0) + entry(pieces, c) * tok
         visible = (key_pos <= pos) & (key_pos >= first_place(pos))
         for h in range(qc // HEAD_WIDTH):
             j = h // group_width
@@ -361,26 +379,26 @@
         ],
         axis=1,
     )
-    cap = cache_out.shape[0]
-    place = jnp.where(
-        lax.broadcasted_iota(jnp.int32, (cap, fsdp_n * per), 0) + 1
-        == slot_line.astype(jnp.int32),
-        1.0, 0.0,
-    ).astype(BF)
-
+    line_out[...] = jnp.broadcast_to(slot_line, line_out.shape)
+
+    def out_copy(which, c):
+        source, target = ((attn_got, attn_out), (got, got_out))[which]
+        return pltpu.make_async_copy(source.at[c], target.at[c], o_sem.at[which, c])
+
+    out_copy(0, ctx).start()
     for step in range(1, ctx_n):
-        a_copy(ctx, (ctx + step) % ctx_n).wait_recv()
-    for c in range(ctx_n):
-        attended_out[:, c * qc : (c + 1) * qc] = attn_got[c]
-
-    @pl.loop(1, total_n)
-    def _(step):
-        c_copy(me, (me + step) % total_n).wait_recv()
-
-    for c in range(ctx_n):
-        rows = jnp.dot(place, got[c], preferred_element_type=F32).astype(BF)
-        cache_out[:, c * kc : (c + 1) * kc] = rows[:, :kc]
-        cache_out[:, (ctx_n + c) * kc : (ctx_n + c + 1) * kc] = rows[:, kc:]
+        sender = (ctx + step) % ctx_n
+        a_copy(ctx, sender).wait_recv()
+        out_copy(0, sender).start()
+
+    for step in range(ctx_n):
+        sender = (ctx + step) % ctx_n
+
+        @pl.loop(1 if step == 0 else 0, fsdp_n)
+        def _(g):
+            c_copy(me, sender * fsdp_n + (fs + g) % fsdp_n).wait_recv()
+
+        out_copy(1, sender).start()
 
     w_sent(0)
     w_sent(1)
@@ -401,6 +419,20 @@
         @pl.when(ctx == 0)
         def _():
             s_copy(to, fs).wait_send()
+
+    for c in range(ctx_n):
+        out_copy(0, c).wait()
+        out_copy(1, c).wait()
+
+
+def place_rows(line, rows, heads, cache, attended, place):
+    @pl.when((pl.program_id(0) == 0) & (pl.program_id(1) == 0))
+    def _():
+        spot = lax.broadcasted_iota(jnp.int32, place.shape, 0) + 1
+        place[...] = jnp.where(spot == line[0:1, :].astype(jnp.int32), 1.0, 0.0).astype(BF)
+
+    attended[...] = heads[0]
+    cache[...] = jnp.dot(place[...], rows[0], preferred_element_type=F32).astype(BF)
 
 
 def shards(
@@ -415,16 +447,18 @@
     stream = ctx_n * tok
     minor_n = fsdp_n // LINE
     vmem = pl.BlockSpec(memory_space=pltpu.VMEM)
-    smem = pl.BlockSpec(memory_space=pltpu.SMEM)
+    anywhere = pl.BlockSpec(memory_space=pl.ANY)
     dma = pltpu.SemaphoreType.DMA
-    attended, cache = pl.pallas_call(
+    cap = total_n * most
+    heads, got, line = pl.pallas_call(
         functools.partial(kernel, ctx_n, fsdp_n, lengths.shape[1]),
         out_shape=(
-            jax.ShapeDtypeStruct((tok, ctx_n * qc), BF),
-            jax.ShapeDtypeStruct((total_n * most, 2 * ctx_n * kc), BF),
+            jax.ShapeDtypeStruct((ctx_n, tok, qc), BF),
+            jax.ShapeDtypeStruct((ctx_n, fsdp_n * per, 2 * kc), BF),
+            jax.ShapeDtypeStruct((8, fsdp_n * per), F32),
         ),
-        in_specs=[smem, smem] + [vmem] * 9,
-        out_specs=(vmem, vmem),
+        in_specs=[vmem] * 11,
+        out_specs=(anywhere, anywhere, vmem),
         scratch_shapes=[
             pltpu.VMEM((stream, width), BF),
             pltpu.VMEM((width, 2 * kc), BF),
@@ -454,15 +488,36 @@
             dma((fsdp_n,)),
             dma((ctx_n,)),
             dma((ctx_n,)),
+            dma((2, ctx_n)),
         ],
         compiler_params=pltpu.CompilerParams(
             collective_id=0, has_side_effects=True, vmem_limit_bytes=56 * 1024 * 1024
         ),
         name="prefill",
     )(
-        lengths, piece_map, hidden[0, 0], norm_gain[None], w_query, w_key, w_value,
+        lengths.T, piece_map.T, hidden[0, 0], norm_gain[None], w_query, w_key, w_value,
         q_gain[None], k_gain[None], owner[0], slot[0],
     )
+    cache, attended = pl.pallas_call(
+        place_rows,
+        out_shape=(
+            jax.ShapeDtypeStruct((cap, 2 * ctx_n * kc), BF),
+            jax.ShapeDtypeStruct((tok, ctx_n * qc), BF),
+        ),
+        grid=(2, ctx_n),
+        in_specs=[
+            pl.BlockSpec((8, fsdp_n * per), lambda half, c: (0, 0)),
+            pl.BlockSpec((1, fsdp_n * per, kc), lambda half, c: (c, 0, half)),
+            pl.BlockSpec((1, tok // 2, qc), lambda half, c: (c, half, 0)),
+        ],
+        out_specs=(
+            pl.BlockSpec((cap, kc), lambda half, c: (0, half * ctx_n + c)),
+            pl.BlockSpec((tok // 2, qc), lambda half, c: (half, c)),
+        ),
+        scratch_shapes=[pltpu.VMEM((cap, fsdp_n * per), BF)],
+        compiler_params=pltpu.CompilerParams(vmem_limit_bytes=56 * 1024 * 1024),
+        name="place_rows",
+    )(line, got, heads)
     return (attended[None, None], cache)
 
 

time: 115 us -> 104 us (0.904)
  local copies, waits for them, and re-layouts: 6.47 us -> 0 us
  Pallas kernels: 107 us -> 104 us
    pallas_call x1, Pallas kernels: 107 us -> 96.5 us  [shards(): pl.pallas_call(functools.partial(kernel, ctx_n, fsdp_n, lengths.shape[1])...]
    pallas_call x0 -> x1, Pallas kernels: none -> 6.98 us  [shards(): pl.pallas_call(place_rows, out_shape=(jax.ShapeDtypeStruct((cap, 2 * ctx_...]
    unnamed x6 -> x0, local copies, waits for them, and re-layouts: 6.47 us -> none
where the time goes in v2:
time: 104 us
  Pallas kernels  104 us (100%)
    pallas_call x1, Pallas kernels, shards(): pl.pallas_call(functools.partial(kernel, ctx_n, fsdp_n, lengths.shape[1])...  96.5 us
    pallas_call x1, Pallas kernels, shards(): pl.pallas_call(place_rows, out_shape=(jax.ShapeDtypeStruct((cap, 2 * ctx_...  6.98 us

profile of v2, /device:TPU:0, one launch (start us, length us, event | category | flops | bytes accessed | tf_op | source)
XLA Modules:
  0.0 104.1 jit_solution(4764776135640910002)
XLA Ops:
  0.6 96.5 %prefill.1 = (bf16[4,256,512]{2,1,0:T(8,128)(2,1)}, bf16[4,512,512]{2,1,0:T(8,128)(2,1)}, f32[8,512]{1,0:T(8,128)}) custom-call(s32[4,8]{1,0:T(4,128)} %bitcast.11, s32[4,8]{1,0:T(4,128)} %bitcast.12, bf16[256,2048]{1,0:T(8,128)(2,1)} %bitcast.9, f32[1,2048]{1,0:T(1,128)} %bitcast.10, bf16[256,512]{1,0:T(8,128)(2,1)} %w_q.1, bf16[256,256]{1,0:T(8,128)(2,1)} %w_k.1, ...), custom_call_target="tpu_custom_call" | custom-call | tf_op jit(solution)/shard_map/prefill/pallas_call | solution.py:453
  97.2 7.0 %place_rows.1 = (bf16[512,2048]{1,0:T(8,128)(2,1)}, bf16[256,2048]{1,0:T(8,128)(2,1)}) custom-call(f32[8,512]{1,0:T(8,128)} %get-tuple-element.7.line, bf16[4,512,512]{2,1,0:T(8,128)(2,1)} %get-tuple-element.8.rows, bf16[4,256,512]{2,1,0:T(8,128)(2,1)} %get-tuple-element.9.heads), custom_call_target="tpu_custom_call" | custom-call | tf_op jit(solution)/shard_map/place_rows/pallas_call | solution.py:501

commit v3 on v2

--- a/solution.py
+++ b/solution.py
@@ -12,6 +12,7 @@
 EPSILON = 1e-06
 THETA = 1000000.0
 NEG_BIG = -1e30
+EXPONENT = math.log2(math.e) / math.sqrt(HEAD_WIDTH)
 MESH = pl.DeviceIdType.MESH
 LINE = 4
 CORES = 2
@@ -282,6 +283,7 @@
             device_id=(to // fsdp_n, to % fsdp_n), device_id_type=MESH,
         )
 
+    w_step(1, 3)
     chunk = 256
     chunks = total_n * per // chunk
     reach = chunk // per
@@ -313,7 +315,6 @@
     def _():
         slot_got[fs] = slot_msg[me]
 
-    w_step(1, 3)
     w_finish(1)
 
     @pl.loop(0, ctx_n)
@@ -353,9 +354,9 @@
             cols = slice(h * HEAD_WIDTH, (h + 1) * HEAD_WIDTH)
             keys = kv[:, j * HEAD_WIDTH : (j + 1) * HEAD_WIDTH]
             values = kv[:, kc + j * HEAD_WIDTH : kc + (j + 1) * HEAD_WIDTH]
-            scores = dot_nt(q_rows[at, cols], keys) * (1.0 / math.sqrt(HEAD_WIDTH))
+            scores = dot_nt(q_rows[at, cols], keys)
             masked = jnp.where(visible, scores, NEG_BIG)
-            weights = jnp.exp(masked - jnp.max(masked, axis=-1, keepdims=True))
+            weights = jnp.exp2((masked - jnp.max(masked, axis=-1, keepdims=True)) * EXPONENT)
             total = jnp.sum(weights, axis=-1, keepdims=True)
             mixed = jnp.dot(weights.astype(BF), values, preferred_element_type=F32)
             attn[at, cols] = (mixed / total).astype(BF)
@@ -425,14 +426,42 @@
         out_copy(1, c).wait()
 
 
-def place_rows(line, rows, heads, cache, attended, place):
-    @pl.when((pl.program_id(0) == 0) & (pl.program_id(1) == 0))
-    def _():
-        spot = lax.broadcasted_iota(jnp.int32, place.shape, 0) + 1
-        place[...] = jnp.where(spot == line[0:1, :].astype(jnp.int32), 1.0, 0.0).astype(BF)
-
-    attended[...] = heads[0]
-    cache[...] = jnp.dot(place[...], rows[0], preferred_element_type=F32).astype(BF)
+def place_rows(
+    line, got, heads, cache, attended, rows, placed, place, in_sem, out_sem, head_sem
+):
+    ctx_n, qc = heads.shape[0], heads.shape[2]
+    kc = got.shape[2] // 2
+
+    def rows_in(c):
+        return pltpu.make_async_copy(got.at[c], rows.at[c], in_sem.at[c])
+
+    def rows_out(c, half):
+        return pltpu.make_async_copy(
+            placed.at[c, :, half * kc : (half + 1) * kc],
+            cache.at[:, (half * ctx_n + c) * kc : (half * ctx_n + c + 1) * kc],
+            out_sem.at[half, c],
+        )
+
+    def heads_across(c):
+        return pltpu.make_async_copy(
+            heads.at[c], attended.at[:, c * qc : (c + 1) * qc], head_sem.at[c]
+        )
+
+    for c in range(ctx_n):
+        rows_in(c).start()
+    for c in range(ctx_n):
+        heads_across(c).start()
+    spot = lax.broadcasted_iota(jnp.int32, place.shape, 0) + 1
+    place[...] = jnp.where(spot == line[0:1, :].astype(jnp.int32), 1.0, 0.0).astype(BF)
+    for c in range(ctx_n):
+        rows_in(c).wait()
+        placed[c] = jnp.dot(place[...], rows[c], preferred_element_type=F32).astype(BF)
+        rows_out(c, 0).start()
+        rows_out(c, 1).start()
+    for c in range(ctx_n):
+        heads_across(c).wait()
+        rows_out(c, 0).wait()
+        rows_out(c, 1).wait()
 
 
 def shards(
@@ -504,17 +533,16 @@
             jax.ShapeDtypeStruct((cap, 2 * ctx_n * kc), BF),
             jax.ShapeDtypeStruct((tok, ctx_n * qc), BF),
         ),
-        grid=(2, ctx_n),
-        in_specs=[
-            pl.BlockSpec((8, fsdp_n * per), lambda half, c: (0, 0)),
-            pl.BlockSpec((1, fsdp_n * per, kc), lambda half, c: (c, 0, half)),
-            pl.BlockSpec((1, tok // 2, qc), lambda half, c: (c, half, 0)),
+        in_specs=[vmem, anywhere, anywhere],
+        out_specs=(anywhere, anywhere),
+        scratch_shapes=[
+            pltpu.VMEM((ctx_n, fsdp_n * per, 2 * kc), BF),
+            pltpu.VMEM((ctx_n, cap, 2 * kc), BF),
+            pltpu.VMEM((cap, fsdp_n * per), BF),
+            dma((ctx_n,)),
+            dma((2, ctx_n)),
+            dma((ctx_n,)),
         ],
-        out_specs=(
-            pl.BlockSpec((cap, kc), lambda half, c: (0, half * ctx_n + c)),
-            pl.BlockSpec((tok // 2, qc), lambda half, c: (half, c)),
-        ),
-        scratch_shapes=[pltpu.VMEM((cap, fsdp_n * per), BF)],
         compiler_params=pltpu.CompilerParams(vmem_limit_bytes=56 * 1024 * 1024),
         name="place_rows",
     )(line, got, heads)

time: 104 us -> 131 us (1.26)
  Pallas kernels: 104 us -> 130 us
    pallas_call x1, Pallas kernels: 6.98 us -> 33.7 us  [shards(): pl.pallas_call(place_rows, out_shape=(jax.ShapeDtypeStruct((cap, 2 * ctx_...]
where the time goes in v3:
time: 131 us
  Pallas kernels  130 us (99%)
    pallas_call x1, Pallas kernels, shards(): pl.pallas_call(functools.partial(kernel, ctx_n, fsdp_n, lengths.shape[1])...  96.3 us
    pallas_call x1, Pallas kernels, shards(): pl.pallas_call(place_rows, out_shape=(jax.ShapeDtypeStruct((cap, 2 * ctx_...  33.7 us

profile of v3, /device:TPU:0, one launch (start us, length us, event | category | flops | bytes accessed | tf_op | source)
XLA Modules:
  0.0 130.7 jit_solution(16393363816869514839)
XLA Ops:
  0.6 96.3 %prefill.1 = (bf16[4,256,512]{2,1,0:T(8,128)(2,1)}, bf16[4,512,512]{2,1,0:T(8,128)(2,1)}, f32[8,512]{1,0:T(8,128)}) custom-call(s32[4,8]{1,0:T(4,128)} %bitcast.11, s32[4,8]{1,0:T(4,128)} %bitcast.12, bf16[256,2048]{1,0:T(8,128)(2,1)} %bitcast.9, f32[1,2048]{1,0:T(1,128)} %bitcast.10, bf16[256,512]{1,0:T(8,128)(2,1)} %w_q.1, bf16[256,256]{1,0:T(8,128)(2,1)} %w_k.1, ...), custom_call_target="tpu_custom_call" | custom-call | tf_op jit(solution)/shard_map/prefill/pallas_call | solution.py:482
  97.0 33.7 %place_rows.1 = (bf16[512,2048]{1,0:T(8,128)(2,1)}, bf16[256,2048]{1,0:T(8,128)(2,1)}) custom-call(f32[8,512]{1,0:T(8,128)} %get-tuple-element.7.line, bf16[4,512,512]{2,1,0:T(8,128)(2,1)} %get-tuple-element.8.got, bf16[4,256,512]{2,1,0:T(8,128)(2,1)} %get-tuple-element.9.heads), custom_call_target="tpu_custom_call" | custom-call | tf_op jit(solution)/shard_map/place_rows/pallas_call | solution.py:530

commit v4 on v3

--- a/solution.py
+++ b/solution.py
@@ -49,6 +49,9 @@
     most = per // ctx_n
     minor_n = fsdp_n // LINE
     rows_y = ctx_n // CORES
+    phases = bucket.shape[0]
+    part = per // phases
+    pair = CORES * tok
     major, minor = fs // minor_n, fs % minor_n
     y_at, core = ctx // CORES, ctx % CORES
     sibling = y_at * CORES + (1 - core)
@@ -193,23 +196,33 @@
         (lane % half).astype(F32) * (-2.0 * math.log(THETA) / HEAD_WIDTH)
     )
 
-    def rope_tables(first, last):
-        @pl.loop(first, last)
-        def _(c):
-            pos = lax.broadcasted_iota(jnp.int32, (tok, HEAD_WIDTH), 0) + entry(pieces, c) * tok
-            angles = (pos - first_place(pos)).astype(F32) * frequency
-            sine = jnp.sin(angles)
-            at = pl.ds(aligned(c, tok), tok)
-            cos_t[at, :] = jnp.cos(angles)
-            sin_t[at, :] = jnp.where(lane < half, -sine, sine)
+    step_angles = lax.broadcasted_iota(jnp.int32, (tok, HEAD_WIDTH), 0).astype(F32) * frequency
+    step_cos, step_sin = jnp.cos(step_angles), jnp.sin(step_angles)
 
     w_step(0, 1)
     w_own(1)
-    rope_tables(0, ctx_n // 2)
+
+    @pl.loop(0, ctx_n)
+    def _(c):
+        start = entry(pieces, c) * tok
+        pos = lax.broadcasted_iota(jnp.int32, (tok, HEAD_WIDTH), 0) + start
+        firsts = [jnp.zeros((1, 1), jnp.int32)] + ends[:-1]
+        shift = jnp.concatenate(
+            [(start - first).astype(F32) * frequency for first in firsts], axis=0
+        )
+        shift_cos, shift_sin = jnp.cos(shift), jnp.sin(shift)
+        row_cos = jnp.broadcast_to(shift_cos[0:1, :], pos.shape)
+        row_sin = jnp.broadcast_to(shift_sin[0:1, :], pos.shape)
+        for j in range(1, seg_n):
+            later = pos >= firsts[j]
+            row_cos = jnp.where(later, shift_cos[j : j + 1, :], row_cos)
+            row_sin = jnp.where(later, shift_sin[j : j + 1, :], row_sin)
+        at = pl.ds(aligned(c, tok), tok)
+        sine = step_sin * row_cos + step_cos * row_sin
+        cos_t[at, :] = step_cos * row_cos - step_sin * row_sin
+        sin_t[at, :] = jnp.where(lane < half, -sine, sine)
+
     w_step(0, 2)
-    rope_tables(ctx_n // 2, ctx_n)
-    w_step(0, 3)
-    w_step(1, 1)
     for step in range(1, ctx_n):
         t_copy((ctx + step) % ctx_n, ctx).wait_recv()
 
@@ -220,15 +233,23 @@
         1.0, 0.0,
     ).astype(BF)
     lane_shift = (fs * per) % HEAD_WIDTH
-    places = []
     slots = jnp.zeros((total_n, HEAD_WIDTH), F32)
-    for c in range(ctx_n):
+
+    def phase_blocks(phase):
+        if phases == 1:
+            return list(range(ctx_n))
+        return [((y_at + phase) % rows_y) * CORES + i for i in range(CORES)]
+
+    places = [[] for _ in range(phases)]
+    for phase, spot, c in [
+        (phase, spot, c) for phase in range(phases) for spot, c in enumerate(phase_blocks(phase))
+    ]:
         owner_row = tab[c, 0:1, :]
         slot_row = tab[c, 1:2, :] + 1
         mine = jnp.where(owners == owner_row, 1.0, 0.0)
         earlier = jnp.dot(mine.astype(BF), before, preferred_element_type=F32)
         rank = jnp.sum(mine * earlier, axis=0, keepdims=True).astype(jnp.int32)
-        places.append(owner_row * per + c * most + rank)
+        places[phase].append(owner_row * part + spot * most + rank)
         column = rank + (c * most + lane_shift)
         spread = jnp.where(
             lax.broadcasted_iota(jnp.int32, (HEAD_WIDTH, tok), 0) == column, 1.0, 0.0
@@ -236,31 +257,20 @@
         high = (mine * (slot_row // 32).astype(F32)).astype(BF)
         low = (mine * (slot_row % 32).astype(F32)).astype(BF)
         slots = slots + dot_nt(high, spread) * 32.0 + dot_nt(low, spread)
-    place_row = jnp.concatenate(places, axis=1)
+    place_rows_of = [jnp.concatenate(found, axis=1) for found in places]
     slot2d[...] = slots
 
     @pl.loop(0, total_n)
     def _(o):
         slot_msg[o] = jnp.broadcast_to(slot2d[pl.ds(o, 1), :], (8, HEAD_WIDTH))
-
-    for step in range(1, rows_y):
-        block = across(step)
-        h_copy(block, sibling, h_send.at[0]).wait_recv()
-        h_copy(block, sibling, f_send.at[block]).start()
-    w_step(1, 2)
-    w_finish(0)
-    h_copy(sibling, sibling, h_send.at[0]).wait_recv()
-    for step in range(1, rows_y):
-        h_copy(((y_at + step) % rows_y) * CORES + 1 - core, sibling, h_send.at[0]).wait_recv()
 
     def norm_rope(x, gain, cosine, sine):
         scale = lax.rsqrt(jnp.mean(x * x, axis=-1, keepdims=True) + EPSILON)
         y = x * scale * gain
         return (y * cosine + pltpu.roll(y, half, 1) * sine).astype(BF)
 
-    @pl.loop(0, ctx_n)
-    def _(c):
-        at = pl.ds(aligned(c, tok), tok)
+    def kv_rows(y):
+        at = pl.ds(aligned(y, pair), pair)
         raw = jnp.dot(normed[at, :], wkv[...], preferred_element_type=F32)
         cosine, sine = cos_t[at, :], sin_t[at, :]
         for h in range(kc // HEAD_WIDTH):
@@ -268,11 +278,13 @@
             kv[at, cols] = norm_rope(raw[:, cols], k_gain[...], cosine, sine)
         kv[at, kc : 2 * kc] = raw[:, kc:].astype(BF)
 
-    def c_copy(to, sender):
+    def c_copy(to, sender, phase):
+        shift = ((sender // (fsdp_n * CORES) + phase) % phases) * part
+        begin = pl.multiple_of((sender % fsdp_n) * per + shift, part)
         return pltpu.make_async_remote_copy(
-            src_ref=bucket.at[pl.ds(aligned(to, per), per), :],
-            dst_ref=got.at[sender // fsdp_n, pl.ds(aligned(sender % fsdp_n, per), per), :],
-            send_sem=c_send.at[to], recv_sem=c_recv.at[sender],
+            src_ref=bucket.at[phase, pl.ds(aligned(to, part), part), :],
+            dst_ref=got.at[sender // fsdp_n, pl.ds(begin, part), :],
+            send_sem=c_send.at[phase, to], recv_sem=c_recv.at[phase, sender],
             device_id=(to // fsdp_n, to % fsdp_n), device_id_type=MESH,
         )
 
@@ -283,33 +295,62 @@
             device_id=(to // fsdp_n, to % fsdp_n), device_id_type=MESH,
         )
 
+    chunk = 256
+    chunks = total_n * part // chunk
+    reach = chunk // part
+    near = reach // 2
+
+    def send_phase(phase):
+        spread = place_rows_of[phase]
+        if phases == 1:
+            tokens = pl.ds(0, ctx_n * tok)
+        else:
+            tokens = pl.ds(aligned((y_at + phase) % rows_y, pair), pair)
+
+        @pl.loop(0, chunks)
+        def _(step):
+            i = (me // reach + 1 + step) % chunks
+            rows = lax.broadcasted_iota(jnp.int32, (chunk, spread.shape[1]), 0) + i * chunk
+            pick = jnp.where(rows == spread, 1.0, 0.0).astype(BF)
+            bucket[phase, pl.ds(aligned(i, chunk), chunk), :] = jnp.dot(
+                pick, kv[tokens, :], preferred_element_type=F32
+            ).astype(BF)
+
+            @pl.loop(0, reach)
+            def _(inner):
+                base = me % reach
+                side = (base // near + 1 + inner // near) % 2
+                to = i * reach + side * near + (base + inner) % near
+
+                @pl.when(to != me)
+                def _():
+                    c_copy(to, me, phase).start()
+
+                    if phase == 0:
+                        @pl.when(ctx == 0)
+                        def _():
+                            s_copy(to, fs).start()
+
+        begin = pl.multiple_of(fs * per + ((y_at + phase) % phases) * part, part)
+        got[ctx, pl.ds(begin, part), :] = bucket[phase, pl.ds(aligned(me, part), part), :]
+
+    w_step(0, 3)
+    w_step(1, 1)
+    w_finish(0)
+    h_copy(sibling, sibling, h_send.at[0]).wait_recv()
+    kv_rows(y_at)
+    for step in range(1, rows_y):
+        block = across(step)
+        h_copy(block, sibling, h_send.at[0]).wait_recv()
+        h_copy(block, sibling, f_send.at[block]).start()
+    w_step(1, 2)
+    if phases == 2:
+        send_phase(0)
+    for step in range(1, rows_y):
+        h_copy(((y_at + step) % rows_y) * CORES + 1 - core, sibling, h_send.at[0]).wait_recv()
+        kv_rows((y_at + step) % rows_y)
     w_step(1, 3)
-    chunk = 256
-    chunks = total_n * per // chunk
-    reach = chunk // per
-
-    @pl.loop(0, chunks)
-    def _(step):
-        i = (me // reach + 1 + 2 * (step % (chunks // 2)) + step // (chunks // 2)) % chunks
-        rows = lax.broadcasted_iota(jnp.int32, (chunk, ctx_n * tok), 0) + i * chunk
-        pick = jnp.where(rows == place_row, 1.0, 0.0).astype(BF)
-        bucket[pl.ds(aligned(i, chunk), chunk), :] = jnp.dot(
-            pick, kv[...], preferred_element_type=F32
-        ).astype(BF)
-
-        @pl.loop(0, reach)
-        def _(inner):
-            to = i * reach + (me + inner) % reach
-
-            @pl.when(to != me)
-            def _():
-                c_copy(to, me).start()
-
-                @pl.when(ctx == 0)
-                def _():
-                    s_copy(to, fs).start()
-
-    got[ctx, pl.ds(aligned(fs, per), per), :] = bucket[pl.ds(aligned(me, per), per), :]
+    send_phase(phases - 1)
 
     @pl.when(ctx == 0)
     def _():
@@ -317,9 +358,9 @@
 
     w_finish(1)
 
-    @pl.loop(0, ctx_n)
-    def _(c):
-        at = pl.ds(aligned(c, tok), tok)
+    @pl.loop(0, rows_y)
+    def _(y):
+        at = pl.ds(aligned(y, pair), pair)
         raw = jnp.dot(normed[at, :], wq[...], preferred_element_type=F32)
         cosine, sine = cos_t[at, :], sin_t[at, :]
         for h in range(qc // HEAD_WIDTH):
@@ -397,7 +438,8 @@
 
         @pl.loop(1 if step == 0 else 0, fsdp_n)
         def _(g):
-            c_copy(me, sender * fsdp_n + (fs + g) % fsdp_n).wait_recv()
+            for phase in range(phases):
+                c_copy(me, sender * fsdp_n + (fs + g) % fsdp_n, phase).wait_recv()
 
         out_copy(1, sender).start()
 
@@ -415,7 +457,8 @@
     @pl.loop(1, total_n)
     def _(step):
         to = (me + step) % total_n
-        c_copy(to, me).wait_send()
+        for phase in range(phases):
+            c_copy(to, me, phase).wait_send()
 
         @pl.when(ctx == 0)
         def _():
@@ -427,7 +470,7 @@
 
 
 def place_rows(
-    line, got, heads, cache, attended, rows, placed, place, in_sem, out_sem, head_sem
+    line, got, heads, cache, attended, rows, placed, held, place, in_sem, out_sem, held_sem, head_sem
 ):
     ctx_n, qc = heads.shape[0], heads.shape[2]
     kc = got.shape[2] // 2
@@ -442,15 +485,18 @@
             out_sem.at[half, c],
         )
 
-    def heads_across(c):
+    def heads_in(c):
+        return pltpu.make_async_copy(heads.at[c], held.at[c], held_sem.at[c])
+
+    def heads_out(c):
         return pltpu.make_async_copy(
-            heads.at[c], attended.at[:, c * qc : (c + 1) * qc], head_sem.at[c]
+            held.at[c], attended.at[:, c * qc : (c + 1) * qc], head_sem.at[c]
         )
 
     for c in range(ctx_n):
         rows_in(c).start()
     for c in range(ctx_n):
-        heads_across(c).start()
+        heads_in(c).start()
     spot = lax.broadcasted_iota(jnp.int32, place.shape, 0) + 1
     place[...] = jnp.where(spot == line[0:1, :].astype(jnp.int32), 1.0, 0.0).astype(BF)
     for c in range(ctx_n):
@@ -458,8 +504,10 @@
         placed[c] = jnp.dot(place[...], rows[c], preferred_element_type=F32).astype(BF)
         rows_out(c, 0).start()
         rows_out(c, 1).start()
+        heads_in(c).wait()
+        heads_out(c).start()
     for c in range(ctx_n):
-        heads_across(c).wait()
+        heads_out(c).wait()
         rows_out(c, 0).wait()
         rows_out(c, 1).wait()
 
@@ -475,6 +523,7 @@
     per = ctx_n * most
     stream = ctx_n * tok
     minor_n = fsdp_n // LINE
+    phases = 2 if ctx_n == 2 * CORES and per // 2 % 16 == 0 else 1
     vmem = pl.BlockSpec(memory_space=pltpu.VMEM)
     anywhere = pl.BlockSpec(memory_space=pl.ANY)
     dma = pltpu.SemaphoreType.DMA
@@ -497,7 +546,7 @@
             pltpu.VMEM((stream, HEAD_WIDTH), F32),
             pltpu.VMEM((stream, 2 * kc), BF),
             pltpu.VMEM((stream, qc), BF),
-            pltpu.VMEM((total_n * per, 2 * kc), BF),
+            pltpu.VMEM((phases, total_n * per // phases, 2 * kc), BF),
             pltpu.VMEM((ctx_n, fsdp_n * per, 2 * kc), BF),
             pltpu.VMEM((total_n, HEAD_WIDTH), F32),
             pltpu.VMEM((total_n, 8, HEAD_WIDTH), F32),
@@ -511,8 +560,8 @@
             dma((ctx_n,)),
             dma((ctx_n,)),
             dma((ctx_n,)),
-            dma((total_n,)),
-            dma((total_n,)),
+            dma((phases, total_n)),
+            dma((phases, total_n)),
             dma((total_n,)),
             dma((fsdp_n,)),
             dma((ctx_n,)),
@@ -538,9 +587,11 @@
         scratch_shapes=[
             pltpu.VMEM((ctx_n, fsdp_n * per, 2 * kc), BF),
             pltpu.VMEM((ctx_n, cap, 2 * kc), BF),
+            pltpu.VMEM((ctx_n, tok, qc), BF),
             pltpu.VMEM((cap, fsdp_n * per), BF),
             dma((ctx_n,)),
             dma((2, ctx_n)),
+            dma((ctx_n,)),
             dma((ctx_n,)),
         ],
         compiler_params=pltpu.CompilerParams(vmem_limit_bytes=56 * 1024 * 1024),

time: 131 us -> 105 us (0.80)
  the two profiles are of different devices: /device:TPU:0 before, /device:TPU:1 now
where the time goes in v4:
time: 105 us; the launch traced here: 104 us
  Pallas kernels  104 us (99%)
    pallas_call x1, Pallas kernels, shards(): pl.pallas_call(functools.partial(kernel, ctx_n, fsdp_n, lengths.shape[1])...  99.1 us
    pallas_call x1, Pallas kernels, shards(): pl.pallas_call(place_rows, out_shape=(jax.ShapeDtypeStruct((cap, 2 * ctx_...  4.58 us

profile of v4, /device:TPU:1, one launch (start us, length us, event | category | flops | bytes accessed | tf_op | source)
XLA Modules:
  0.0 104.3 jit_solution(5499445294055702647)
XLA Ops:
  0.6 99.1 %prefill.1 = (bf16[4,256,512]{2,1,0:T(8,128)(2,1)}, bf16[4,512,512]{2,1,0:T(8,128)(2,1)}, f32[8,512]{1,0:T(8,128)}) custom-call(s32[4,8]{1,0:T(4,128)} %bitcast.11, s32[4,8]{1,0:T(4,128)} %bitcast.12, bf16[256,2048]{1,0:T(8,128)(2,1)} %bitcast.9, f32[1,2048]{1,0:T(1,128)} %bitcast.10, bf16[256,512]{1,0:T(8,128)(2,1)} %w_q.1, bf16[256,256]{1,0:T(8,128)(2,1)} %w_k.1, ...), custom_call_target="tpu_custom_call" | custom-call | tf_op jit(solution)/shard_map/prefill/pallas_call | solution.py:531
  99.7 4.6 %place_rows.1 = (bf16[512,2048]{1,0:T(8,128)(2,1)}, bf16[256,2048]{1,0:T(8,128)(2,1)}) custom-call(f32[8,512]{1,0:T(8,128)} %get-tuple-element.7.line, bf16[4,512,512]{2,1,0:T(8,128)(2,1)} %get-tuple-element.8.got, bf16[4,256,512]{2,1,0:T(8,128)(2,1)} %get-tuple-element.9.heads), custom_call_target="tpu_custom_call" | custom-call | tf_op jit(solution)/shard_map/place_rows/pallas_call | solution.py:579

commit v5 on v3

--- a/solution.py
+++ b/solution.py
@@ -49,6 +49,7 @@
     most = per // ctx_n
     minor_n = fsdp_n // LINE
     rows_y = ctx_n // CORES
+    pair = CORES * tok
     major, minor = fs // minor_n, fs % minor_n
     y_at, core = ctx // CORES, ctx % CORES
     sibling = y_at * CORES + (1 - core)
@@ -193,23 +194,33 @@
         (lane % half).astype(F32) * (-2.0 * math.log(THETA) / HEAD_WIDTH)
     )
 
-    def rope_tables(first, last):
-        @pl.loop(first, last)
-        def _(c):
-            pos = lax.broadcasted_iota(jnp.int32, (tok, HEAD_WIDTH), 0) + entry(pieces, c) * tok
-            angles = (pos - first_place(pos)).astype(F32) * frequency
-            sine = jnp.sin(angles)
-            at = pl.ds(aligned(c, tok), tok)
-            cos_t[at, :] = jnp.cos(angles)
-            sin_t[at, :] = jnp.where(lane < half, -sine, sine)
+    step_angles = lax.broadcasted_iota(jnp.int32, (tok, HEAD_WIDTH), 0).astype(F32) * frequency
+    step_cos, step_sin = jnp.cos(step_angles), jnp.sin(step_angles)
 
     w_step(0, 1)
     w_own(1)
-    rope_tables(0, ctx_n // 2)
+
+    @pl.loop(0, ctx_n)
+    def _(c):
+        start = entry(pieces, c) * tok
+        pos = lax.broadcasted_iota(jnp.int32, (tok, HEAD_WIDTH), 0) + start
+        firsts = [jnp.zeros((1, 1), jnp.int32)] + ends[:-1]
+        shift = jnp.concatenate(
+            [(start - first).astype(F32) * frequency for first in firsts], axis=0
+        )
+        shift_cos, shift_sin = jnp.cos(shift), jnp.sin(shift)
+        row_cos = jnp.broadcast_to(shift_cos[0:1, :], pos.shape)
+        row_sin = jnp.broadcast_to(shift_sin[0:1, :], pos.shape)
+        for j in range(1, seg_n):
+            later = pos >= firsts[j]
+            row_cos = jnp.where(later, shift_cos[j : j + 1, :], row_cos)
+            row_sin = jnp.where(later, shift_sin[j : j + 1, :], row_sin)
+        at = pl.ds(aligned(c, tok), tok)
+        sine = step_sin * row_cos + step_cos * row_sin
+        cos_t[at, :] = step_cos * row_cos - step_sin * row_sin
+        sin_t[at, :] = jnp.where(lane < half, -sine, sine)
+
     w_step(0, 2)
-    rope_tables(ctx_n // 2, ctx_n)
-    w_step(0, 3)
-    w_step(1, 1)
     for step in range(1, ctx_n):
         t_copy((ctx + step) % ctx_n, ctx).wait_recv()
 
@@ -220,8 +231,9 @@
         1.0, 0.0,
     ).astype(BF)
     lane_shift = (fs * per) % HEAD_WIDTH
+    slots = jnp.zeros((total_n, HEAD_WIDTH), F32)
+
     places = []
-    slots = jnp.zeros((total_n, HEAD_WIDTH), F32)
     for c in range(ctx_n):
         owner_row = tab[c, 0:1, :]
         slot_row = tab[c, 1:2, :] + 1
@@ -243,6 +255,37 @@
     def _(o):
         slot_msg[o] = jnp.broadcast_to(slot2d[pl.ds(o, 1), :], (8, HEAD_WIDTH))
 
+    def norm_rope(x, gain, cosine, sine):
+        scale = lax.rsqrt(jnp.mean(x * x, axis=-1, keepdims=True) + EPSILON)
+        y = x * scale * gain
+        return (y * cosine + pltpu.roll(y, half, 1) * sine).astype(BF)
+
+    def kv_rows(y):
+        at = pl.ds(aligned(y, pair), pair)
+        raw = jnp.dot(normed[at, :], wkv[...], preferred_element_type=F32)
+        cosine, sine = cos_t[at, :], sin_t[at, :]
+        for h in range(kc // HEAD_WIDTH):
+            cols = slice(h * HEAD_WIDTH, (h + 1) * HEAD_WIDTH)
+            kv[at, cols] = norm_rope(raw[:, cols], k_gain[...], cosine, sine)
+        kv[at, kc : 2 * kc] = raw[:, kc:].astype(BF)
+
+    def c_copy(to, sender):
+        return pltpu.make_async_remote_copy(
+            src_ref=bucket.at[pl.ds(aligned(to, per), per), :],
+            dst_ref=got.at[sender // fsdp_n, pl.ds(aligned(sender % fsdp_n, per), per), :],
+            send_sem=c_send.at[to], recv_sem=c_recv.at[sender],
+            device_id=(to // fsdp_n, to % fsdp_n), device_id_type=MESH,
+        )
+
+    def s_copy(to, sender):
+        return pltpu.make_async_remote_copy(
+            src_ref=slot_msg.at[to], dst_ref=slot_got.at[sender],
+            send_sem=s_send.at[to], recv_sem=s_recv.at[sender],
+            device_id=(to // fsdp_n, to % fsdp_n), device_id_type=MESH,
+        )
+
+    w_step(0, 3)
+    w_step(1, 1)
     for step in range(1, rows_y):
         block = across(step)
         h_copy(block, sibling, h_send.at[0]).wait_recv()
@@ -250,40 +293,12 @@
     w_step(1, 2)
     w_finish(0)
     h_copy(sibling, sibling, h_send.at[0]).wait_recv()
+    kv_rows(y_at)
     for step in range(1, rows_y):
         h_copy(((y_at + step) % rows_y) * CORES + 1 - core, sibling, h_send.at[0]).wait_recv()
-
-    def norm_rope(x, gain, cosine, sine):
-        scale = lax.rsqrt(jnp.mean(x * x, axis=-1, keepdims=True) + EPSILON)
-        y = x * scale * gain
-        return (y * cosine + pltpu.roll(y, half, 1) * sine).astype(BF)
-
-    @pl.loop(0, ctx_n)
-    def _(c):
-        at = pl.ds(aligned(c, tok), tok)
-        raw = jnp.dot(normed[at, :], wkv[...], preferred_element_type=F32)
-        cosine, sine = cos_t[at, :], sin_t[at, :]
-        for h in range(kc // HEAD_WIDTH):
-            cols = slice(h * HEAD_WIDTH, (h + 1) * HEAD_WIDTH)
-            kv[at, cols] = norm_rope(raw[:, cols], k_gain[...], cosine, sine)
-        kv[at, kc : 2 * kc] = raw[:, kc:].astype(BF)
-
-    def c_copy(to, sender):
-        return pltpu.make_async_remote_copy(
-            src_ref=bucket.at[pl.ds(aligned(to, per), per), :],
-            dst_ref=got.at[sender // fsdp_n, pl.ds(aligned(sender % fsdp_n, per), per), :],
-            send_sem=c_send.at[to], recv_sem=c_recv.at[sender],
-            device_id=(to // fsdp_n, to % fsdp_n), device_id_type=MESH,
-        )
-
-    def s_copy(to, sender):
-        return pltpu.make_async_remote_copy(
-            src_ref=slot_msg.at[to], dst_ref=slot_got.at[sender],
-            send_sem=s_send.at[to], recv_sem=s_recv.at[sender],
-            device_id=(to // fsdp_n, to % fsdp_n), device_id_type=MESH,
-        )
-
+        kv_rows((y_at + step) % rows_y)
     w_step(1, 3)
+
     chunk = 256
     chunks = total_n * per // chunk
     reach = chunk // per
@@ -317,9 +332,9 @@
 
     w_finish(1)
 
-    @pl.loop(0, ctx_n)
-    def _(c):
-        at = pl.ds(aligned(c, tok), tok)
+    @pl.loop(0, rows_y)
+    def _(y):
+        at = pl.ds(aligned(y, pair), pair)
         raw = jnp.dot(normed[at, :], wq[...], preferred_element_type=F32)
         cosine, sine = cos_t[at, :], sin_t[at, :]
         for h in range(qc // HEAD_WIDTH):
@@ -427,7 +442,7 @@
 
 
 def place_rows(
-    line, got, heads, cache, attended, rows, placed, place, in_sem, out_sem, head_sem
+    line, got, heads, cache, attended, rows, placed, held, place, in_sem, out_sem, held_sem, head_sem
 ):
     ctx_n, qc = heads.shape[0], heads.shape[2]
     kc = got.shape[2] // 2
@@ -442,15 +457,18 @@
             out_sem.at[half, c],
         )
 
-    def heads_across(c):
+    def heads_in(c):
+        return pltpu.make_async_copy(heads.at[c], held.at[c], held_sem.at[c])
+
+    def heads_out(c):
         return pltpu.make_async_copy(
-            heads.at[c], attended.at[:, c * qc : (c + 1) * qc], head_sem.at[c]
+            held.at[c], attended.at[:, c * qc : (c + 1) * qc], head_sem.at[c]
         )
 
     for c in range(ctx_n):
         rows_in(c).start()
     for c in range(ctx_n):
-        heads_across(c).start()
+        heads_in(c).start()
     spot = lax.broadcasted_iota(jnp.int32, place.shape, 0) + 1
     place[...] = jnp.where(spot == line[0:1, :].astype(jnp.int32), 1.0, 0.0).astype(BF)
     for c in range(ctx_n):
@@ -458,8 +476,10 @@
         placed[c] = jnp.dot(place[...], rows[c], preferred_element_type=F32).astype(BF)
         rows_out(c, 0).start()
         rows_out(c, 1).start()
+        heads_in(c).wait()
+        heads_out(c).start()
     for c in range(ctx_n):
-        heads_across(c).wait()
+        heads_out(c).wait()
         rows_out(c, 0).wait()
         rows_out(c, 1).wait()
 
@@ -538,9 +558,11 @@
         scratch_shapes=[
             pltpu.VMEM((ctx_n, fsdp_n * per, 2 * kc), BF),
             pltpu.VMEM((ctx_n, cap, 2 * kc), BF),
+            pltpu.VMEM((ctx_n, tok, qc), BF),
             pltpu.VMEM((cap, fsdp_n * per), BF),
             dma((ctx_n,)),
             dma((2, ctx_n)),
+            dma((ctx_n,)),
             dma((ctx_n,)),
         ],
         compiler_params=pltpu.CompilerParams(vmem_limit_bytes=56 * 1024 * 1024),

time: 131 us -> 104 us (0.79)
  Pallas kernels: 130 us -> 103 us
    pallas_call x1, Pallas kernels: 33.7 us -> 4.58 us  [shards(): pl.pallas_call(place_rows, out_shape=(jax.ShapeDtypeStruct((cap, 2 * ctx_...]
    pallas_call x1, Pallas kernels: 96.3 us -> 98.7 us  [shards(): pl.pallas_call(functools.partial(kernel, ctx_n, fsdp_n, lengths.shape[1])...]
where the time goes in v5:
time: 104 us
  Pallas kernels  103 us (99%)
    pallas_call x1, Pallas kernels, shards(): pl.pallas_call(functools.partial(kernel, ctx_n, fsdp_n, lengths.shape[1])...  98.7 us
    pallas_call x1, Pallas kernels, shards(): pl.pallas_call(place_rows, out_shape=(jax.ShapeDtypeStruct((cap, 2 * ctx_...  4.58 us

profile of v5, /device:TPU:0, one launch (start us, length us, event | category | flops | bytes accessed | tf_op | source)
XLA Modules:
  0.0 103.9 jit_solution(881821664800323347)
XLA Ops:
  0.6 98.7 %prefill.1 = (bf16[4,256,512]{2,1,0:T(8,128)(2,1)}, bf16[4,512,512]{2,1,0:T(8,128)(2,1)}, f32[8,512]{1,0:T(8,128)}) custom-call(s32[4,8]{1,0:T(4,128)} %bitcast.11, s32[4,8]{1,0:T(4,128)} %bitcast.12, bf16[256,2048]{1,0:T(8,128)(2,1)} %bitcast.9, f32[1,2048]{1,0:T(1,128)} %bitcast.10, bf16[256,512]{1,0:T(8,128)(2,1)} %w_q.1, bf16[256,256]{1,0:T(8,128)(2,1)} %w_k.1, ...), custom_call_target="tpu_custom_call" | custom-call | tf_op jit(solution)/shard_map/prefill/pallas_call | solution.py:502
  99.4 4.6 %place_rows.1 = (bf16[512,2048]{1,0:T(8,128)(2,1)}, bf16[256,2048]{1,0:T(8,128)(2,1)}) custom-call(f32[8,512]{1,0:T(8,128)} %get-tuple-element.7.line, bf16[4,512,512]{2,1,0:T(8,128)(2,1)} %get-tuple-element.8.got, bf16[4,256,512]{2,1,0:T(8,128)(2,1)} %get-tuple-element.9.heads), custom_call_target="tpu_custom_call" | custom-call | tf_op jit(solution)/shard_map/place_rows/pallas_call | solution.py:550
